TPU v7x, 256 devices: a whole 4x4x8 slice. The times are simulated.
256 devices in a mesh: rx: 4 (over z_hi, core), ry: 4 (over x), fsdp: 16 (over y, z_lo).
Axes of the slice: x: 4, y: 4, z: 8 (z_hi: 2, z_lo: 4; z = z_hi * 4 + z_lo), core: 2. Of those that a mesh axis runs over, the one named last changes fastest.
Arguments:
- inputs: bfloat16 [4, 4, 2, 2048, 4096], P('rx', 'ry', None, 'fsdp'), may hold values from -6 to 6
- value_grad: bfloat16 [4, 4, 2, 2048, 1024], P('rx', 'ry', None, 'fsdp'), may hold values from -0.099609375 to 0.099609375
- weight: float32 [4, 4, 4096, 1024], P('rx', 'ry', 'fsdp'), may hold values from -6 to 6
- weight_m: float32 [4, 4, 4096, 1024], P('rx', 'ry', 'fsdp'), may hold values from -3 to 3
- weight_v: float32 [4, 4, 4096, 1024], P('rx', 'ry', 'fsdp'), may hold values from 0.001 to 0.1
- gain: float32 [4, 4, 4096], P('rx', 'ry', 'fsdp'), may hold values from 0.5 to 1.5
- gain_m: float32 [4, 4, 4096], P('rx', 'ry', 'fsdp'), may hold values from -3 to 3
- gain_v: float32 [4, 4, 4096], P('rx', 'ry', 'fsdp'), may hold values from 0.001 to 0.1
- mixing: int32 [4, 4, 5], P('rx', 'ry'), may hold values from 1 to 8
Outputs:
- input_grad: float32 [4, 4, 2, 2048, 4096], P('rx', 'ry', None, 'fsdp')
- new_weight: float32 [4, 4, 4096, 1024], P('rx', 'ry', 'fsdp')
- new_weight_m: float32 [4, 4, 4096, 1024], P('rx', 'ry', 'fsdp')
- new_weight_v: float32 [4, 4, 4096, 1024], P('rx', 'ry', 'fsdp')
- new_gain: float32 [4, 4, 4096], P('rx', 'ry', 'fsdp')
- new_gain_m: float32 [4, 4, 4096], P('rx', 'ry', 'fsdp')
- new_gain_v: float32 [4, 4, 4096], P('rx', 'ry', 'fsdp')
All inputs are finite; a program needn't handle non-finite values.
Results may differ from a plain program's by a relative error of at most 0.0042.
Values may be sent and summed in bfloat16 or wider, within the bound.
A program may use at most 128 MiB of HBM per device.

v0:
```python
import jax
import jax.numpy as jnp
from jax import lax
from jax.sharding import PartitionSpec as P


def with_halo(value, sides, width):
    for axis, dim in sides:
        devices, length = (lax.axis_size(axis), value.shape[dim])
        up = [(i, (i + 1) % devices) for i in range(devices)]
        down = [(j, i) for i, j in up]
        last = lax.slice_in_dim(value, length - width, length, axis=dim)
        leading = lax.slice_in_dim(value, 0, width, axis=dim)
        before = lax.ppermute(last, axis, up)
        after = lax.ppermute(leading, axis, down)
        value = jnp.concatenate([before, value, after], axis=dim)
    return value


def gather_params(own_weight, own_gain_low):
    return (
        lax.all_gather(own_weight.astype(jnp.bfloat16), "fsdp", axis=0, tiled=True),
        lax.all_gather(own_gain_low, "fsdp", axis=0, tiled=True),
    )


def backward_rows(flat_cot, own_weight, own_gain_low):
    full_weight, full_gain = gather_params(own_weight, own_gain_low)
    out_grad = lax.dot_general(
        flat_cot, full_weight, (((1,), (1,)), ((), ())), preferred_element_type=jnp.float32
    )
    return (out_grad, full_gain)


def body(inputs, value_grad, weight, weight_m, weight_v, gain, gain_m, gain_v, mixing):
    padded_weight, padded_gain = (
        with_halo(weight, (("rx", 0), ("ry", 1)), 1),
        with_halo(gain, (("rx", 0), ("ry", 1)), 1),
    )
    count_rows = inputs.shape[2] * inputs.shape[3]
    width = inputs.shape[4]
    flat_acts = inputs[0, 0].reshape(count_rows, width).astype(jnp.float32)
    flat_cot = value_grad[0, 0].reshape(count_rows, value_grad.shape[4])
    own_weight = weight[0, 0]
    own_gain = gain[0, 0]
    own_gain_low = own_gain.astype(jnp.bfloat16)
    scale = lax.rsqrt(jnp.mean(flat_acts * flat_acts, axis=1, keepdims=True) + 1e-05)
    unit = flat_acts * scale
    normalized = unit.astype(jnp.bfloat16)
    out_grad, full_gain = backward_rows(flat_cot, own_weight, own_gain_low)
    gain_term = jnp.sum(out_grad * unit, axis=0)
    term = lax.dot_general(
        normalized, flat_cot, (((0,), (0,)), ((), ())), preferred_element_type=jnp.float32
    )
    summed, grad_gain = (
        lax.psum_scatter(term, "fsdp", scatter_dimension=0, tiled=True),
        lax.psum_scatter(gain_term, "fsdp", scatter_dimension=0, tiled=True),
    )
    unit_grad = out_grad * full_gain.astype(jnp.float32)[None, :]
    inner = jnp.mean(unit_grad * unit, axis=1, keepdims=True)
    input_grad = scale * (unit_grad - unit * inner)
    grad_weight = own_gain_low.astype(jnp.float32)[:, None] * summed
    new_wm = 0.9 * weight_m[0, 0] + 0.1 * grad_weight
    new_wv = 0.999 * weight_v[0, 0] + 0.001 * grad_weight * grad_weight
    stepped_w = own_weight - 0.01 * (new_wm / (jnp.sqrt(new_wv) + 1e-08) + 0.1 * own_weight)
    new_gm = 0.9 * gain_m[0, 0] + 0.1 * grad_gain
    new_gv = 0.999 * gain_v[0, 0] + 0.001 * grad_gain * grad_gain
    stepped_g = own_gain - 0.01 * new_gm / (jnp.sqrt(new_gv) + 1e-08)
    raw_share = mixing[0, 0].astype(jnp.float32)
    share = raw_share / jnp.sum(raw_share)

    def mixed(stepped, padded):
        total = share[0] * stepped
        total = total + share[1] * padded[0, 1]
        total = total + share[2] * padded[2, 1]
        total = total + share[3] * padded[1, 0]
        total = total + share[4] * padded[1, 2]
        return total

    new_weight = mixed(stepped_w, padded_weight)
    new_gain = mixed(stepped_g, padded_gain)
    return (
        input_grad.reshape(inputs.shape),
        new_weight[None, None],
        new_wm[None, None],
        new_wv[None, None],
        new_gain[None, None],
        new_gm[None, None],
        new_gv[None, None],
    )


def solution(mesh):
    placed = (
        P("rx", "ry", None, "fsdp", None),
        P("rx", "ry", None, "fsdp", None),
        P("rx", "ry", "fsdp", None),
        P("rx", "ry", "fsdp", None),
        P("rx", "ry", "fsdp", None),
        P("rx", "ry", "fsdp"),
        P("rx", "ry", "fsdp"),
        P("rx", "ry", "fsdp"),
        P("rx", "ry", None),
    )
    return jax.shard_map(
        body,
        mesh=mesh,
        in_specs=placed,
        out_specs=(
            P("rx", "ry", None, "fsdp", None),
            P("rx", "ry", "fsdp", None),
            P("rx", "ry", "fsdp", None),
            P("rx", "ry", "fsdp", None),
            P("rx", "ry", "fsdp"),
            P("rx", "ry", "fsdp"),
            P("rx", "ry", "fsdp"),
        ),
        check_vma=False,
    )
```

profile of v0, /device:TPU:1, one launch (start us, length us, event | category | flops | bytes accessed | tf_op | source)
XLA Modules:
  0.0 628.0 jit_solution(17588229525800554551)
XLA Ops:
  7.2 8.4 %collective-permute-start = (f32[1,1,256,1024]{3,2,1,0:T(8,128)}, f32[1,1,256,1024]{3,2,1,0:T(8,128)S(1)}, u32[]{:S(2)}, u32[]{:S(2)}) collective-permute-start(f32[1,1,256,1024]{3,2,1,0:T(8,128)} %param.11), channel_id=1, source_target_pairs={{0,64},{64,128},{128,192},{192,0},{1,65},{65,129},{129,193},{193,1... | collective-permute-start | bytes 3145736 | tf_op jit(solution)/shard_map/ppermute | solution.py:14
  15.6 14.4 %collective-permute-done = f32[1,1,256,1024]{3,2,1,0:T(8,128)S(1)} collective-permute-done((f32[1,1,256,1024]{3,2,1,0:T(8,128)}, f32[1,1,256,1024]{3,2,1,0:T(8,128)S(1)}, u32[]{:S(2)}, u32[]{:S(2)}) %collective-permute-start) | collective-permute-done | bytes 1048608 | tf_op jit(solution)/shard_map/ppermute | solution.py:14
  30.0 1.0 copy-done.2
  31.0 1.1 constant_dynamic-update-slice_fusion.2
  32.1 2.5 constant_dynamic-update-slice_fusion.1
  35.2 8.2 %convolution_bitcast_fusion = f32[4096,1024]{1,0:T(8,128)} fusion(bf16[1,1,2,128,4096]{4,3,2,1,0:T(8,128)(2,1)S(1)} %copy-done.1, f32[2,128]{1,0:T(2,128)S(1)} %get-tuple-element.23, bf16[1,1,2,128,1024]{4,3,2,1,0:T(8,128)(2,1)S(1)} %copy-done), kind=kOutput, calls=%fused_computation | convolution fusion | flops 2150629376 | bytes 19399680 | tf_op jit(solution)/shard_map/dot_general | solution.py:52
  43.5 1.3 collective-permute-start.1
  45.3 5.2 collective-permute-start.4
  51.1 0.6 convert_divide_fusion
  51.8 0.7 fusion.19
  53.1 10.0 %collective-permute-done.1 = f32[1,1,256,1024]{3,2,1,0:T(8,128)S(1)} collective-permute-done((f32[1,1,256,1024]{3,2,1,0:T(8,128)}, f32[1,1,256,1024]{3,2,1,0:T(8,128)S(1)}, u32[]{:S(2)}, u32[]{:S(2)}) %collective-permute-start.1) | collective-permute-done | bytes 1048608 | tf_op jit(solution)/shard_map/ppermute | solution.py:15
  63.1 1.0 copy-done.3
  64.1 1.1 constant_dynamic-update-slice_fusion
  65.2 38.3 %collective-permute-start.3 = (f32[3,1,256,1024]{3,2,1,0:T(8,128)}, f32[3,1,256,1024]{3,2,1,0:T(8,128)}, u32[]{:S(2)}, u32[]{:S(2)}) collective-permute-start(f32[3,1,256,1024]{3,2,1,0:T(8,128)} %constant_dynamic-update-slice_fusion), channel_id=1, source_target_pairs={{16,0},{32,16},{48,32},{0,48},{17,1},{33,17},{49,33},{1,49},{18,2}... | collective-permute-start | bytes 9437192 | tf_op jit(solution)/shard_map/ppermute | solution.py:15
  104.1 2.8 collective-permute-start.7
  106.8 58.3 %all-gather = bf16[16,1,256]{2,1,0:T(2,128)(2,1)S(1)} all-gather(bf16[1,1,256]{2,1,0:T(2,128)(2,1)S(1)} %reshape.102), channel_id=1, replica_groups=mesh['rx'=4,'ry'=4,'fsdp'=16] {'fsdp'}, dimensions={0}, use_global_device_ids=true | all-gather | bytes 8704 | tf_op jit(solution)/shard_map/all_gather | solution.py:23
  167.3 3.0 collective-permute-done.6
  170.9 77.0 %all-gather.3.cloned.1.call-done = bf16[4096,1024]{1,0:T(8,128)(2,1)} async-done(((bf16[256,1024]{1,0:T(8,128)(2,1)}), bf16[4096,1024]{1,0:T(8,128)(2,1)}) %all-gather.3.cloned.1.call-update) | async-done | bytes 8388624 | tf_op jit(solution)/shard_map/all_gather | solution.py:22
  247.9 8.3 %multiply_reduce_fusion = (f32[4096]{0:T(1024)S(1)}, f32[256]{0:T(256)S(1)}, f32[256,4096]{1,0:T(8,128)}) fusion(bf16[1,1,2,128,4096]{4,3,2,1,0:T(8,128)(2,1)S(1)} %copy-done.1, f32[256]{0:T(256)S(1)} %get-tuple-element.24, f32[4096]{0:T(1024)S(1)} %bitcast.93, bf16[256,1024]{1,0:T(8,128)(2,1)S(1)} %bitcast.91, ...), kind=kOutput, calls=%fused_computation.2 | convolution fusion | flops 2154819328 | bytes 15239168 | tf_op jit(solution)/shard_map/dot_general | solution.py:29
  256.2 66.3 %all-reduce = f32[4096]{0:T(1024)S(1)} all-reduce(f32[4096]{0:T(1024)S(1)} %get-tuple-element.7), channel_id=3, replica_groups=mesh['rx'=4,'ry'=4,'fsdp'=16] {'fsdp'}, use_global_device_ids=true, to_apply=%region_5.0.clone | all-reduce | flops 4096 | bytes 32768
  322.6 1.3 add_add_fusion
  323.8 5.3 subtract_multiply_fusion
  329.1 282.5 %reduce-scatter.2.cloned.1.call-done = f32[256,1024]{1,0:T(8,128)} async-done(((f32[4096,1024]{1,0:T(8,128)}), f32[256,1024]{1,0:T(8,128)}) %reduce-scatter.2.cloned.1.call-update) | async-done | bytes 1048592 | tf_op jit(solution)/shard_map/reduce_scatter | solution.py:56
  611.6 9.5 %fusion.15 = (f32[1,1,256,1024]{3,2,1,0:T(8,128)}, f32[1,1,256,1024]{3,2,1,0:T(8,128)}, f32[1,1,256,1024]{3,2,1,0:T(8,128)}) fusion(f32[256,1024]{1,0:T(8,128)} %reduce-scatter.2.cloned.1.call-done, f32[256]{0:T(256)S(1)} %get-tuple-element.12, f32[1,1,256,1024]{3,2,1,0:T(8,128)} %param.13, f32[3,1,256,1024]{3,2,1,0:T(8,128)} %collective-permute-done.3, ...), kind=kLoop, calls=%fused_computation.49 | loop fusion | flops 6029312 | bytes 11535380 | tf_op jit(solution)/shard_map/broadcast_in_dim | solution.py:86
  (43 shorter events, 5.2 us)
Async XLA Ops:
  7.2 28.0 %copy-start = (bf16[1,1,2,128,1024]{4,3,2,1,0:T(8,128)(2,1)S(1)}, bf16[1,1,2,128,1024]{4,3,2,1,0:T(8,128)(2,1)}, u32[]{:S(2)}) copy-start(bf16[1,1,2,128,1024]{4,3,2,1,0:T(8,128)(2,1)} %param.10) | copy-start | bytes 1572868
  7.2 27.5 %copy-start.1 = (bf16[1,1,2,128,4096]{4,3,2,1,0:T(8,128)(2,1)S(1)}, bf16[1,1,2,128,4096]{4,3,2,1,0:T(8,128)(2,1)}, u32[]{:S(2)}) copy-start(bf16[1,1,2,128,4096]{4,3,2,1,0:T(8,128)(2,1)} %param.9) | copy-start | bytes 6291460
  7.2 240.8 %all-gather.3.cloned.1.call-start = ((), (), s32[]{:S(2)}) async-start(), calls=%async_computation.1 | async-start | bytes 8912896 | tf_op jit(solution)/shard_map/all_gather | solution.py:22
  7.2 22.8 %collective-permute-start = (f32[1,1,256,1024]{3,2,1,0:T(8,128)}, f32[1,1,256,1024]{3,2,1,0:T(8,128)S(1)}, u32[]{:S(2)}, u32[]{:S(2)}) collective-permute-start(f32[1,1,256,1024]{3,2,1,0:T(8,128)} %param.11), channel_id=1, source_target_pairs={{0,64},{64,128},{128,192},{192,0},{1,65},{65,129},{129,193},{193,1... | collective-permute-start | bytes 3145736 | tf_op jit(solution)/shard_map/ppermute | solution.py:14
  30.0 1.0 copy-start.2
  34.6 577.0 %reduce-scatter.2.cloned.1.call-start = ((), (), s32[]{:S(2)}) async-start(), calls=%async_computation.2 | async-start | bytes 17825792 | tf_op jit(solution)/shard_map/reduce_scatter | solution.py:56
  43.4 1.3 copy-start.4
  43.4 7.1 %copy-start.7 = (s32[1,1,5]{2,1,0:T(1,128)S(1)}, s32[1,1,5]{2,1,0:T(1,128)}, u32[]{:S(2)}) copy-start(s32[1,1,5]{2,1,0:T(1,128)} %param.17) | copy-start | bytes 64
  43.4 7.7 %copy-start.5 = (f32[1,1,256]{2,1,0:T(1,128)S(1)}, f32[1,1,256]{2,1,0:T(1,128)}, u32[]{:S(2)}) copy-start(f32[1,1,256]{2,1,0:T(1,128)} %param.15) | copy-start | bytes 3076
  43.4 8.3 %copy-start.6 = (f32[1,1,256]{2,1,0:T(1,128)S(1)}, f32[1,1,256]{2,1,0:T(1,128)}, u32[]{:S(2)}) copy-start(f32[1,1,256]{2,1,0:T(1,128)} %param.16) | copy-start | bytes 3076
  43.4 121.7 %copy-start.8 = (u32[256]{0:T(256)S(1)}, u32[256]{0:T(256)}, u32[]{:S(2)}) copy-start(u32[256]{0:T(256)} %constant.37) | copy-start | bytes 3076
  43.5 19.6 %collective-permute-start.1 = (f32[1,1,256,1024]{3,2,1,0:T(8,128)}, f32[1,1,256,1024]{3,2,1,0:T(8,128)S(1)}, u32[]{:S(2)}, u32[]{:S(2)}) collective-permute-start(f32[1,1,256,1024]{3,2,1,0:T(8,128)} %param.11), channel_id=1, source_target_pairs={{64,0},{128,64},{192,128},{0,192},{65,1},{129,65},{193,129},{1,193... | collective-permute-start | bytes 3145736 | tf_op jit(solution)/shard_map/ppermute | solution.py:15
  44.8 58.7 %collective-permute-start.5 = (f32[1,1,256]{2,1,0:T(1,128)S(1)}, f32[1,1,256]{2,1,0:T(1,128)S(1)}, u32[]{:S(2)}, u32[]{:S(2)}) collective-permute-start(f32[1,1,256]{2,1,0:T(1,128)S(1)} %copy-done.4), channel_id=1, source_target_pairs={{64,0},{128,64},{192,128},{0,192},{65,1},{129,65},{193,129},{1,193... | collective-permute-start | bytes 3080 | tf_op jit(solution)/shard_map/ppermute | solution.py:15
  45.3 7.1 %collective-permute-start.4 = (f32[1,1,256]{2,1,0:T(1,128)S(1)}, f32[1,1,256]{2,1,0:T(1,128)S(1)}, u32[]{:S(2)}, u32[]{:S(2)}) collective-permute-start(f32[1,1,256]{2,1,0:T(1,128)S(1)} %copy-done.4), channel_id=1, source_target_pairs={{0,64},{64,128},{128,192},{192,0},{1,65},{65,129},{129,193},{193,1... | collective-permute-start | bytes 3080 | tf_op jit(solution)/shard_map/ppermute | solution.py:14
  63.1 1.0 copy-start.3
  65.2 263.9 %collective-permute-start.3 = (f32[3,1,256,1024]{3,2,1,0:T(8,128)}, f32[3,1,256,1024]{3,2,1,0:T(8,128)}, u32[]{:S(2)}, u32[]{:S(2)}) collective-permute-start(f32[3,1,256,1024]{3,2,1,0:T(8,128)} %constant_dynamic-update-slice_fusion), channel_id=1, source_target_pairs={{16,0},{32,16},{48,32},{0,48},{17,1},{33,17},{49,33},{1,49},{18,2}... | collective-permute-start | bytes 9437192 | tf_op jit(solution)/shard_map/ppermute | solution.py:15
  103.4 225.7 %collective-permute-start.2 = (f32[3,1,256,1024]{3,2,1,0:T(8,128)}, f32[3,1,256,1024]{3,2,1,0:T(8,128)}, u32[]{:S(2)}, u32[]{:S(2)}) collective-permute-start(f32[3,1,256,1024]{3,2,1,0:T(8,128)} %constant_dynamic-update-slice_fusion), channel_id=1, source_target_pairs={{0,16},{16,32},{32,48},{48,0},{1,17},{17,33},{33,49},{49,1},{2,18}... | collective-permute-start | bytes 9437192 | tf_op jit(solution)/shard_map/ppermute | solution.py:14
  104.1 62.6 %collective-permute-start.7 = (f32[3,1,256]{2,1,0:T(1,128)S(1)}, f32[3,1,256]{2,1,0:T(1,128)S(1)}, u32[]{:S(2)}, u32[]{:S(2)}) collective-permute-start(f32[3,1,256]{2,1,0:T(1,128)S(1)} %get-tuple-element.22), channel_id=1, source_target_pairs={{16,0},{32,16},{48,32},{0,48},{17,1},{33,17},{49,33},{1,49},{18,2}... | collective-permute-start | bytes 9224 | tf_op jit(solution)/shard_map/ppermute | solution.py:15
  166.4 3.9 collective-permute-start.6
Sparse Core Ops, SparseCore 0:
  34.7 213.1 all-gather.2
  250.5 361.0 reduce-scatter.1
where the time goes:
time: 628 us
  waiting for transfers between devices  387 us (62%)
  blocking collectives  125 us (20%)
  starting transfers between devices  56.8 us (9%)
  other arithmetic  22.9 us (4%)
  matrix products  16.5 us (3%)
  between operations  14.8 us (2%)
    reduce_scatter x1, waiting for transfers between devices, body(): lax.psum_scatter(term, 'fsdp', scatter_dimension=0, tiled=True)  282 us
    all_gather x1, waiting for transfers between devices, gather_params(): lax.all_gather(own_weight.astype(jnp.bfloat16), 'fsdp', axis=0, tiled=True)  77 us
    unnamed x1, blocking collectives  66.3 us
    all_gather x1, blocking collectives, gather_params(): lax.all_gather(own_gain_low, 'fsdp', axis=0, tiled=True)  58.3 us
    ppermute x4, starting transfers between devices, with_halo(): after = lax.ppermute(leading, axis, down)  42.9 us
    ppermute x4, waiting for transfers between devices, with_halo(): before = lax.ppermute(last, axis, up)  17.4 us
    ppermute x4, starting transfers between devices, with_halo(): before = lax.ppermute(last, axis, up)  13.8 us
  transfers between devices with their start and end apart: 10, of which 5 were waited for; matrix products, arithmetic and copies ran while one was open for 5% of the time, Pallas kernels for 0%

commit v1 on v0

v1 whole, which is shorter than its diff:
```python
import jax
import jax.numpy as jnp
from jax import lax
from jax.experimental import pallas as pl
from jax.experimental.pallas import tpu as pltpu
from jax.sharding import PartitionSpec as P

MESH = pl.DeviceIdType.MESH
F32 = jnp.float32
BF16 = jnp.bfloat16

ROWS = 256
BLK = 256
KV = 1024
WIDE = 1024
WROWS = BLK + 16

VG = 0
WL = 6
WR = 10
NS = 14
US = 26
RR = 38
RL = 42
GG = 46
GO = 49
NSEM = 53


def step_kernel(
    mix, x_hbm, vg_hbm, w_hbm, m_hbm, v_hbm, gain, gain_m, gain_v,
    ig, nw, nm, nv, ng, ngm, ngv,
    xv, wf, mv, vv, vgp, nown, npool, npt, wp, us, ur, gbuf, rsend, rr, rl, gg, ggr, gos, sc, gcol,
    lsem, ssem, rsem,
):
    rx = lax.axis_index("rx")
    ry = lax.axis_index("ry")
    f = lax.axis_index("fsdp")
    zh = rx // 2
    core = rx % 2
    y = f // 4
    z = f % 4

    def dev(yy, zz):
        return (rx, ry, yy * 4 + zz)

    def ypeer(r):
        return dev((y + r) % 4, z)

    far_rx = (1 - zh) * 2 + (1 - core)
    chip_rx = zh * 2 + (1 - core)

    def remote(src, dst, k, device):
        return pltpu.make_async_remote_copy(
            src_ref=src, dst_ref=dst, send_sem=ssem.at[k], recv_sem=rsem.at[k],
            device_id=device, device_id_type=MESH,
        )

    loads = [
        pltpu.make_async_copy(w_hbm, wf, lsem.at[0]),
        pltpu.make_async_copy(x_hbm, xv, lsem.at[1]),
        pltpu.make_async_copy(vg_hbm, vgp.at[pl.ds(0, ROWS)], lsem.at[2]),
        pltpu.make_async_copy(m_hbm, mv, lsem.at[3]),
        pltpu.make_async_copy(v_hbm, vv, lsem.at[4]),
    ]
    for c in loads:
        c.start()

    barrier = pltpu.get_barrier_semaphore()
    far_base = (1 - z // 2) * 2
    partners = [ypeer(1), ypeer(2), ypeer(3)]
    partners += [dev(y, (z + 1) % 4), dev(y, (z + 2) % 4), dev(y, (z + 3) % 4)]
    partners += [(rx, (ry + 1) % 4, f), (rx, (ry + 3) % 4, f), (chip_rx, ry, f)]
    partners += [(far_rx, ry, y * 4 + far_base), (far_rx, ry, y * 4 + far_base + 1)]
    for p in partners:
        pl.semaphore_signal(barrier, inc=1, device_id=p, device_id_type=MESH)
    pl.semaphore_wait(barrier, len(partners))

    sent = []

    def go(copy, cond=None):
        copy.start()
        sent.append((cond, copy))

    def half(ref, slot, h):
        return ref.at[pl.ds(slot * ROWS + h * (ROWS // 2), ROWS // 2)]

    go(remote(half(vg_hbm, 0, 0), half(vgp, 1, 0), VG + 0, ypeer(1)))
    go(remote(half(vg_hbm, 0, 1), half(vgp, 3, 1), VG + 1, ypeer(3)))
    go(remote(half(vg_hbm, 0, 1), half(vgp, 1, 1), VG + 2, ypeer(1)))
    go(remote(half(vg_hbm, 0, 0), half(vgp, 3, 0), VG + 3, ypeer(3)))

    loads[0].wait()
    gain_row = gain[0].astype(BF16)

    def cast_rows(i, carry):
        rows = pl.ds(pl.multiple_of(i * 32, 32), 32)
        wp[z, rows, :] = wf[rows, :].astype(BF16)
        return carry

    lax.fori_loop(0, BLK // 32, cast_rows, 0)
    wp[z, BLK:WROWS, :] = jnp.zeros((16, KV), BF16)
    wp[z, BLK:WROWS, 0:BLK] = jnp.broadcast_to(gain_row.astype(F32), (16, BLK)).astype(BF16)

    def wright(s):
        return remote(wp.at[z - s], wp.at[z - s], WL + s, dev(y, z + 1))

    def wleft(s):
        return remote(wp.at[z + s], wp.at[z + s], WR + s, dev(y, z - 1))

    @pl.when(z < 3)
    def _():
        wright(0).start()

    @pl.when(z > 0)
    def _():
        wleft(0).start()

    go(remote(wp.at[z], gos.at[2], GO + 2, (chip_rx, ry, f)))
    go(remote(wp.at[z], gos.at[0], GO + 0, (rx, (ry + 1) % 4, f)))
    go(remote(wp.at[z], gos.at[1], GO + 1, (rx, (ry + 3) % 4, f)))

    def far(zz):
        return remote(wp.at[zz], gos.at[3], GO + 3, (far_rx, ry, y * 4 + zz))

    loads[1].wait()

    def norm_rows(i, carry):
        rows = pl.ds(pl.multiple_of(i * 16, 16), 16)
        x = xv[rows, :].astype(F32)
        s = lax.rsqrt(jnp.sum(x * x, axis=1, keepdims=True) * (1.0 / 4096) + 1e-05)
        sc[rows, :] = jnp.broadcast_to(s, (16, 128))
        n = (x * s).astype(BF16)
        for yy in range(4):
            for b in range(4):
                at = yy * WIDE + b * BLK
                nown[yy, b, rows, :] = n[:, at:at + BLK]
        return carry

    lax.fori_loop(0, ROWS // 16, norm_rows, 0)

    remote(half(vg_hbm, 0, 0), half(vgp, 1, 0), VG + 0, ypeer(1)).wait_recv()
    go(remote(half(vgp, 1, 0), half(vgp, 2, 0), VG + 4, ypeer(1)))
    remote(half(vg_hbm, 0, 1), half(vgp, 3, 1), VG + 1, ypeer(3)).wait_recv()
    go(remote(half(vgp, 3, 1), half(vgp, 2, 1), VG + 5, ypeer(3)))

    upper = z // 2
    near = z + upper * (3 - 2 * z)

    def order(i):
        t = ((27 + 72 * near) // 4**i) % 4
        return t + upper * (3 - 2 * t)

    def slot(r):
        return pl.ds(r * ROWS, ROWS)

    def ncopy(i, r):
        b = order(i)
        return remote(nown.at[(y + r) % 4, b], npool.at[b, slot(r)], NS + 3 * i + r - 1, ypeer(r))

    for i in range(4):
        for r in (1, 3, 2):
            go(ncopy(i, r))

    def own_rows(i, carry):
        rows = pl.ds(pl.multiple_of(i * 64, 64), 64)
        for b in range(4):
            npool[b, rows, :] = nown[y, b, rows, :]
        return carry

    lax.fori_loop(0, ROWS // 64, own_rows, 0)

    def weights_arrive(s):
        @pl.when(z - s >= 0)
        def _():
            remote(wp.at[z - s], wp.at[z - s], WL + s - 1, dev(y, z)).wait_recv()

            @pl.when(z < 3)
            def _():
                wright(s).start()

        @pl.when(z + s <= 3)
        def _():
            remote(wp.at[z + s], wp.at[z + s], WR + s - 1, dev(y, z)).wait_recv()

            @pl.when(z > 0)
            def _():
                wleft(s).start()

        if s >= 2:
            @pl.when(z == 3)
            def _():
                far(3 - s).start()

            @pl.when(z == 0)
            def _():
                far(s).start()

    def rsright(b):
        return remote(rsend.at[b], rr.at[b], RR + b, dev(y, z + 1))

    def rsleft(b):
        return remote(rsend.at[b], rl.at[b], RL + b, dev(y, z - 1))

    def round_block(b, other=None):
        def rows_body(i, carry):
            rows = pl.ds(pl.multiple_of(i * 32, 32), 32)
            g = gbuf[b, rows, :]
            if other is not None:
                g = g + other[b, rows, :].astype(F32)
            rsend[b, rows, :] = g.astype(BF16)
            return carry

        lax.fori_loop(0, BLK // 32, rows_body, 0)

    def weight_grad(i):
        b = order(i)
        for r in (1, 3, 2):
            ncopy(i, r).wait_recv()
        npt[...] = npool[b].T

        def columns(c, carry):
            cols = pl.ds(pl.multiple_of(c * 256, 256), 256)
            gbuf[b, :, cols] = jnp.dot(npt[...], vgp[:, cols], preferred_element_type=F32)
            return carry

        lax.fori_loop(0, KV // 256, columns, 0)
        if i < 3:
            @pl.when(z == 0)
            def _():
                round_block(3 - i)
                rsright(3 - i).start()

            @pl.when(z == 3)
            def _():
                round_block(i)
                rsleft(i).start()

    def ucopy(i, r):
        b = order(i)
        return remote(us.at[b, slot(r)], ur.at[y, b], US + 3 * i + r - 1, ypeer(4 - r))

    def unit_grad(i):
        b = order(i)
        gl = wp[b, BLK:WROWS, 0:BLK].astype(F32)[0:1, :]

        def tokens(r, acc):
            rows = pl.ds(pl.multiple_of(r * ROWS, ROWS), ROWS)
            og = lax.dot_general(
                vgp[rows, :], wp[b, 0:BLK, :], (((1,), (1,)), ((), ())), preferred_element_type=F32
            )
            us[b, rows, :] = (og * gl).astype(BF16)
            prod = og * npool[b, rows, :].astype(F32)
            return acc + jnp.sum(prod.reshape(ROWS // 8, 8, BLK), axis=0)

        gg[b] = lax.fori_loop(0, 4, tokens, jnp.zeros((8, BLK), F32))
        for r in (1, 3, 2):
            go(ucopy(i, r))
        ur[y, b] = us[b, 0:ROWS, :]

    weights_arrive(1)
    loads[2].wait()
    for k, (s, h) in ((4, (2, 0)), (5, (2, 1)), (2, (1, 1)), (3, (3, 0))):
        remote(half(vgp, s, h), half(vgp, s, h), VG + k, ypeer(1)).wait_recv()
    weight_grad(0)
    weights_arrive(2)
    weight_grad(1)
    weight_grad(2)
    weights_arrive(3)

    def forward_right(b):
        remote(rsend.at[b], rr.at[b], RR + b, dev(y, z)).wait_recv()
        round_block(b, rr)
        rsright(b).start()

    def forward_left(b):
        remote(rsend.at[b], rl.at[b], RL + b, dev(y, z)).wait_recv()
        round_block(b, rl)
        rsleft(b).start()

    unit_grad(0)
    unit_grad(1)

    @pl.when(z == 1)
    def _():
        forward_right(3)

    @pl.when(z == 2)
    def _():
        forward_left(0)

    unit_grad(2)
    weight_grad(3)
    unit_grad(3)

    def ggcopy(d):
        zz = (z + d) % 4
        return remote(gg.at[zz], ggr.at[d - 1], GG + d - 1, dev(y, zz))

    for d in (1, 2, 3):
        go(ggcopy(d))

    @pl.when(z == 1)
    def _():
        forward_right(2)
        forward_left(0)

    @pl.when(z == 2)
    def _():
        forward_left(1)
        forward_right(3)

    total = (mix[0, 0, 0] + mix[0, 0, 1] + mix[0, 0, 2] + mix[0, 0, 3] + mix[0, 0, 4]).astype(F32)

    def share(n, width):
        return jnp.full((1, width), mix[0, 0, n].astype(F32), F32) / jnp.full((1, width), total, F32)

    from_chip, from_far = 2 - core, 1 + core

    for d in (1, 2, 3):
        ggcopy(d).wait_recv()
    g8 = gg[z] + ggr[0] + ggr[1] + ggr[2]
    grad_gain = jnp.sum(g8, axis=0, keepdims=True)
    own_gain = gain[0]
    new_gm = 0.9 * gain_m[0] + 0.1 * grad_gain
    new_gv = 0.999 * gain_v[0] + 0.001 * grad_gain * grad_gain
    ngm[0] = new_gm
    ngv[0] = new_gv
    stepped_g = own_gain - 0.01 * new_gm / (jnp.sqrt(new_gv) + 1e-08)

    remote(gos.at[2], gos.at[2], GO + 2, dev(y, z)).wait_recv()
    remote(gos.at[0], gos.at[0], GO + 0, dev(y, z)).wait_recv()
    remote(gos.at[1], gos.at[1], GO + 1, dev(y, z)).wait_recv()
    remote(gos.at[3], gos.at[3], GO + 3, dev(y, z)).wait_recv()

    def gossip_gain(n):
        return gos[n, BLK:WROWS, 0:BLK].astype(F32)[0:1, :]

    mixed_g = share(0, BLK) * stepped_g
    mixed_g = mixed_g + share(3, BLK) * gossip_gain(0) + share(4, BLK) * gossip_gain(1)
    mixed_g = mixed_g + share(from_chip, BLK) * gossip_gain(2) + share(from_far, BLK) * gossip_gain(3)
    ng[0] = mixed_g

    eye = lax.broadcasted_iota(jnp.int32, (BLK, BLK), 0) == lax.broadcasted_iota(jnp.int32, (BLK, BLK), 1)
    col = jnp.sum(jnp.where(eye, jnp.broadcast_to(gain_row.astype(F32), (BLK, BLK)), 0.0), axis=1, keepdims=True)
    gcol[...] = jnp.broadcast_to(col, (BLK, 128))

    def add_block(other):
        def rows_body(i, carry):
            rows = pl.ds(pl.multiple_of(i * 32, 32), 32)
            gbuf[z, rows, :] = gbuf[z, rows, :] + other[z, rows, :].astype(F32)
            return carry

        lax.fori_loop(0, BLK // 32, rows_body, 0)

    @pl.when(z > 0)
    def _():
        remote(rsend.at[z], rr.at[z], RR + z, dev(y, z)).wait_recv()
        add_block(rr)

    @pl.when(z < 3)
    def _():
        remote(rsend.at[z], rl.at[z], RL + z, dev(y, z)).wait_recv()
        add_block(rl)

    loads[3].wait()
    loads[4].wait()
    s0, s1, s2 = share(0, KV), share(3, KV), share(4, KV)
    s3, s4 = share(from_chip, KV), share(from_far, KV)

    def adam_rows(i, carry):
        rows = pl.ds(pl.multiple_of(i * 16, 16), 16)
        g = gcol[rows, 0:1] * gbuf[z, rows, :]
        new_m = 0.9 * mv[rows, :] + 0.1 * g
        new_v = 0.999 * vv[rows, :] + 0.001 * g * g
        nm[rows, :] = new_m
        nv[rows, :] = new_v
        own = wf[rows, :]
        stepped = own - 0.01 * (new_m / (jnp.sqrt(new_v) + 1e-08) + 0.1 * own)
        out = s0 * stepped + s1 * gos[0, rows, :].astype(F32) + s2 * gos[1, rows, :].astype(F32)
        nw[rows, :] = out + s3 * gos[2, rows, :].astype(F32) + s4 * gos[3, rows, :].astype(F32)
        return carry

    lax.fori_loop(0, BLK // 16, adam_rows, 0)

    for i in range(4):
        for r in (1, 3, 2):
            ucopy(i, r).wait_recv()

    def grad_rows(i, carry):
        rows = pl.ds(pl.multiple_of(i * 16, 16), 16)
        s = sc[rows, 0:1]
        inner = jnp.zeros((16, 1), F32)
        for yy in range(4):
            for b in range(4):
                at = yy * WIDE + b * BLK
                unit = xv[rows, at:at + BLK].astype(F32) * s
                inner = inner + jnp.sum(ur[yy, b, rows, :].astype(F32) * unit, axis=1, keepdims=True)
        inner = inner * (1.0 / 4096)
        for yy in range(4):
            for b in range(4):
                at = yy * WIDE + b * BLK
                unit = xv[rows, at:at + BLK].astype(F32) * s
                ig[rows, at:at + BLK] = s * (ur[yy, b, rows, :].astype(F32) - unit * inner)
        return carry

    lax.fori_loop(0, ROWS // 16, grad_rows, 0)

    for _, copy in sent:
        copy.wait_send()
    for s in range(3):
        @pl.when((z < 3) & (z - s >= 0))
        def _():
            wright(s).wait_send()

        @pl.when((z > 0) & (z + s <= 3))
        def _():
            wleft(s).wait_send()

    for s in (2, 3):
        @pl.when(z == 3)
        def _():
            far(3 - s).wait_send()

        @pl.when(z == 0)
        def _():
            far(s).wait_send()

    for b in range(4):
        @pl.when(z < b)
        def _():
            rsright(b).wait_send()

        @pl.when(z > b)
        def _():
            rsleft(b).wait_send()


def body(inputs, value_grad, weight, weight_m, weight_v, gain, gain_m, gain_v, mixing):
    vmem = pl.BlockSpec(memory_space=pltpu.VMEM)
    hbm = pl.BlockSpec(memory_space=pl.ANY)
    outs = pl.pallas_call(
        step_kernel,
        name="gossip_step",
        out_shape=[
            jax.ShapeDtypeStruct((ROWS, 4 * WIDE), F32),
            jax.ShapeDtypeStruct((BLK, KV), F32),
            jax.ShapeDtypeStruct((BLK, KV), F32),
            jax.ShapeDtypeStruct((BLK, KV), F32),
            jax.ShapeDtypeStruct((1, 1, BLK), F32),
            jax.ShapeDtypeStruct((1, 1, BLK), F32),
            jax.ShapeDtypeStruct((1, 1, BLK), F32),
        ],
        in_specs=[pl.BlockSpec(memory_space=pltpu.SMEM)] + [hbm] * 5 + [vmem] * 3,
        out_specs=[vmem] * 7,
        scratch_shapes=[
            pltpu.VMEM((ROWS, 4 * WIDE), BF16),
            pltpu.VMEM((BLK, KV), F32),
            pltpu.VMEM((BLK, KV), F32),
            pltpu.VMEM((BLK, KV), F32),
            pltpu.VMEM((4 * ROWS, KV), BF16),
            pltpu.VMEM((4, 4, ROWS, BLK), BF16),
            pltpu.VMEM((4, 4 * ROWS, BLK), BF16),
            pltpu.VMEM((BLK, 4 * ROWS), BF16),
            pltpu.VMEM((4, WROWS, KV), BF16),
            pltpu.VMEM((4, 4 * ROWS, BLK), BF16),
            pltpu.VMEM((4, 4, ROWS, BLK), BF16),
            pltpu.VMEM((4, BLK, KV), F32),
            pltpu.VMEM((4, BLK, KV), BF16),
            pltpu.VMEM((4, BLK, KV), BF16),
            pltpu.VMEM((4, BLK, KV), BF16),
            pltpu.VMEM((4, 8, BLK), F32),
            pltpu.VMEM((3, 8, BLK), F32),
            pltpu.VMEM((4, WROWS, KV), BF16),
            pltpu.VMEM((ROWS, 128), F32),
            pltpu.VMEM((BLK, 128), F32),
            pltpu.SemaphoreType.DMA((5,)),
            pltpu.SemaphoreType.DMA((NSEM,)),
            pltpu.SemaphoreType.DMA((NSEM,)),
        ],
        compiler_params=pltpu.CompilerParams(
            collective_id=0, has_side_effects=True, vmem_limit_bytes=56 << 20
        ),
    )(
        mixing,
        inputs.reshape(ROWS, 4 * WIDE),
        value_grad.reshape(ROWS, KV),
        weight[0, 0],
        weight_m[0, 0],
        weight_v[0, 0],
        gain,
        gain_m,
        gain_v,
    )
    ig, nw, nm, nv, ng, ngm, ngv = outs
    return (ig.reshape(inputs.shape), nw[None, None], nm[None, None], nv[None, None], ng, ngm, ngv)


def solution(mesh):
    placed = (
        P("rx", "ry", None, "fsdp", None),
        P("rx", "ry", None, "fsdp", None),
        P("rx", "ry", "fsdp", None),
        P("rx", "ry", "fsdp", None),
        P("rx", "ry", "fsdp", None),
        P("rx", "ry", "fsdp"),
        P("rx", "ry", "fsdp"),
        P("rx", "ry", "fsdp"),
        P("rx", "ry", None),
    )
    return jax.shard_map(
        body,
        mesh=mesh,
        in_specs=placed,
        out_specs=(
            P("rx", "ry", None, "fsdp", None),
            P("rx", "ry", "fsdp", None),
            P("rx", "ry", "fsdp", None),
            P("rx", "ry", "fsdp", None),
            P("rx", "ry", "fsdp"),
            P("rx", "ry", "fsdp"),
            P("rx", "ry", "fsdp"),
        ),
        check_vma=False,
    )
```

time: 628 us -> 106 us (0.17)
  waiting for transfers between devices: 387 us -> 0 us
  blocking collectives: 125 us -> 0 us
  Pallas kernels: 0 us -> 96.1 us
  starting transfers between devices: 56.8 us -> 0 us
  other arithmetic: 22.9 us -> 0 us
  matrix products: 16.5 us -> 0 us
  between operations: 14.8 us -> 0.68 us
    reduce_scatter x1 -> x0, waiting for transfers between devices: 282 us -> none  [body(): lax.psum_scatter(term, 'fsdp', scatter_dimension=0, tiled=True)]
    pallas_call x0 -> x1, Pallas kernels: none -> 96.1 us  [body(): pl.pallas_call(step_kernel, name='gossip_step', out_shape=[jax.ShapeDtype...]
    all_gather x1 -> x0, waiting for transfers between devices: 77 us -> none  [gather_params(): lax.all_gather(own_weight.astype(jnp.bfloat16), 'fsdp', axis=0, tiled=True)]
    unnamed x1 -> x0, blocking collectives: 66.3 us -> none
    all_gather x1 -> x0, blocking collectives: 58.3 us -> none  [gather_params(): lax.all_gather(own_gain_low, 'fsdp', axis=0, tiled=True)]
    ppermute x8 -> x0, starting transfers between devices: 56.7 us -> none  [the longest x4 42.9 us: with_halo(): after = lax.ppermute(leading, axis, down)]
    ppermute x8 -> x0, waiting for transfers between devices: 27.4 us -> none  [the longest x4 17.4 us: with_halo(): before = lax.ppermute(last, axis, up)]
    dot_general x2 -> x0, matrix products: 16.5 us -> none  [the longest x1 8.27 us: backward_rows(): lax.dot_general(flat_cot, full_weight, (((1,), (1,)), ((), ())), preferre...]
  transfers between devices with their start and end apart: 10 -> 0, of which waited for: 5 -> 0; matrix products, arithmetic and copies ran while one was open for 5% -> 0% of each run, Pallas kernels for 0% -> 0%
where the time goes in v1:
time: 106 us
  Pallas kernels  96.1 us (91%)
  local copies, waits for them, and re-layouts  9.42 us (9%)
    pallas_call x1, Pallas kernels, body(): pl.pallas_call(step_kernel, name='gossip_step', out_shape=[jax.ShapeDtype...  96.1 us
    unnamed x19, local copies, waits for them, and re-layouts  9.42 us

profile of v1, /device:TPU:1, one launch (start us, length us, event | category | flops | bytes accessed | tf_op | source)
XLA Modules:
  0.0 106.2 jit_solution(6039797891067627772)
XLA Ops:
  0.6 96.1 %gossip_step.1 = (f32[256,4096]{1,0:T(8,128)}, f32[256,1024]{1,0:T(8,128)}, f32[256,1024]{1,0:T(8,128)}, f32[256,1024]{1,0:T(8,128)}, f32[1,1,256]{2,1,0:T(1,128...) custom-call(s32[1,1,5]{2,1,0:T(1,128)} %mix.1, bf16[256,4096]{1,0:T(8,128)(2,1)} %bitcast.10, bf16[256,1024]{1,0:T(8,128)(2,1)} %bitcast.17, ...), custom_call_target="tpu_custom_call" | custom-call | tf_op jit(solution)/shard_map/gossip_step/pallas_call | solution.py:442
  96.7 0.0 copy-start.2
  96.7 0.0 copy-start.1
  96.8 4.8 %copy.23 = f32[1,1,2,128,4096]{4,3,2,1,0:T(8,128)} copy(f32[1,1,2,128,4096]{4,3,2,1,0:T(8,128)} %bitcast.9) | data formatting | bytes 8388608
  101.6 0.0 copy-done.2
  101.6 0.0 copy-start
  101.6 0.0 copy-start.5
  101.6 0.0 copy-start.4
  101.6 0.0 copy-start.3
  101.6 1.0 copy.24
  102.6 0.0 copy-done.1
  102.6 1.0 copy.25
  103.5 0.0 copy-done
  103.5 1.0 copy.26
  104.5 0.0 copy-done.5
  104.5 0.6 copy.27
  105.1 0.0 copy-done.4
  105.1 0.6 copy.28
  105.6 0.0 copy-done.3
  105.6 0.6 copy.29
Async XLA Ops:
  96.7 4.8 %copy-start.2 = (f32[256,1024]{1,0:T(8,128)S(1)}, f32[256,1024]{1,0:T(8,128)}, u32[]{:S(2)}) copy-start(f32[256,1024]{1,0:T(8,128)} %get-tuple-element.15) | copy-start | bytes 3145732
  96.7 5.8 %copy-start.1 = (f32[256,1024]{1,0:T(8,128)S(1)}, f32[256,1024]{1,0:T(8,128)}, u32[]{:S(2)}) copy-start(f32[256,1024]{1,0:T(8,128)} %get-tuple-element.16) | copy-start | bytes 3145732
  101.6 2.0 %copy-start = (f32[256,1024]{1,0:T(8,128)S(1)}, f32[256,1024]{1,0:T(8,128)}, u32[]{:S(2)}) copy-start(f32[256,1024]{1,0:T(8,128)} %get-tuple-element.17) | copy-start | bytes 3145732
  101.6 2.9 %copy-start.5 = (f32[1,1,256]{2,1,0:T(1,128)S(1)}, f32[1,1,256]{2,1,0:T(1,128)}, u32[]{:S(2)}) copy-start(f32[1,1,256]{2,1,0:T(1,128)} %get-tuple-element.32) | copy-start | bytes 3076
  101.6 3.5 %copy-start.4 = (f32[1,1,256]{2,1,0:T(1,128)S(1)}, f32[1,1,256]{2,1,0:T(1,128)}, u32[]{:S(2)}) copy-start(f32[1,1,256]{2,1,0:T(1,128)} %get-tuple-element.33) | copy-start | bytes 3076
  101.6 4.1 %copy-start.3 = (f32[1,1,256]{2,1,0:T(1,128)S(1)}, f32[1,1,256]{2,1,0:T(1,128)}, u32[]{:S(2)}) copy-start(f32[1,1,256]{2,1,0:T(1,128)} %get-tuple-element.34) | copy-start | bytes 3076

commit v2 on v1

--- a/solution.py
+++ b/solution.py
@@ -17,21 +17,27 @@
 
 VG = 0
 WL = 6
-WR = 10
-NS = 14
-US = 26
-RR = 38
-RL = 42
-GG = 46
-GO = 49
-NSEM = 53
+WR = 14
+NS = 22
+US = 34
+RR = 46
+RL = 54
+GG = 62
+GO = 65
+NSEM = 70
+
+
+def KC(k):
+    for lo, c in ((65, "GO"), (62, "GG"), (46, "RS"), (34, "US"), (22, "NS"), (6, "W"), (0, "VG")):
+        if k >= lo:
+            return c
 
 
 def step_kernel(
     mix, x_hbm, vg_hbm, w_hbm, m_hbm, v_hbm, gain, gain_m, gain_v,
-    ig, nw, nm, nv, ng, ngm, ngv,
-    xv, wf, mv, vv, vgp, nown, npool, npt, wp, us, ur, gbuf, rsend, rr, rl, gg, ggr, gos, sc, gcol,
-    lsem, ssem, rsem,
+    ur, nw, nm, nv, ng, ngm, ngv,
+    xv, wf, mv, vv, vgp, nown, npool, npt, wp, us, gbuf, rsend, rr, rl, gg, ggr, gos, gcol,
+    lsem, osem, ssem, rsem,
 ):
     rx = lax.axis_index("rx")
     ry = lax.axis_index("ry")
@@ -102,26 +108,45 @@
     wp[z, BLK:WROWS, :] = jnp.zeros((16, KV), BF16)
     wp[z, BLK:WROWS, 0:BLK] = jnp.broadcast_to(gain_row.astype(F32), (16, BLK)).astype(BF16)
 
-    def wright(s):
-        return remote(wp.at[z - s], wp.at[z - s], WL + s, dev(y, z + 1))
-
-    def wleft(s):
-        return remote(wp.at[z + s], wp.at[z + s], WR + s, dev(y, z - 1))
+    def whalf(block, h):
+        return wp.at[block, pl.ds(h * 128, 128 + 16 * h)]
+
+    def wright(s, h):
+        return remote(whalf(z - s, h), whalf(z - s, h), WL + 2 * s + h, dev(y, z + 1))
+
+    def wleft(s, h):
+        return remote(whalf(z + s, h), whalf(z + s, h), WR + 2 * s + h, dev(y, z - 1))
+
+    def from_left(s, h):
+        remote(whalf(z - s, h), whalf(z - s, h), WL + 2 * s + h - 2, dev(y, z)).wait_recv()
+
+    def from_right(s, h):
+        remote(whalf(z + s, h), whalf(z + s, h), WR + 2 * s + h - 2, dev(y, z)).wait_recv()
+
+    def far(zz, h):
+        return remote(
+            whalf(zz, h), gos.at[3, pl.ds(h * 128, 128 + 16 * h)], GO + 3 + h,
+            (far_rx, ry, y * 4 + zz))
 
     @pl.when(z < 3)
     def _():
-        wright(0).start()
+        wright(0, 0).start()
 
     @pl.when(z > 0)
     def _():
-        wleft(0).start()
+        wleft(0, 0).start()
+
+    @pl.when(z < 2)
+    def _():
+        wright(0, 1).start()
+
+    @pl.when(z > 1)
+    def _():
+        wleft(0, 1).start()
 
     go(remote(wp.at[z], gos.at[2], GO + 2, (chip_rx, ry, f)))
     go(remote(wp.at[z], gos.at[0], GO + 0, (rx, (ry + 1) % 4, f)))
     go(remote(wp.at[z], gos.at[1], GO + 1, (rx, (ry + 3) % 4, f)))
-
-    def far(zz):
-        return remote(wp.at[zz], gos.at[3], GO + 3, (far_rx, ry, y * 4 + zz))
 
     loads[1].wait()
 
@@ -129,7 +154,6 @@
         rows = pl.ds(pl.multiple_of(i * 16, 16), 16)
         x = xv[rows, :].astype(F32)
         s = lax.rsqrt(jnp.sum(x * x, axis=1, keepdims=True) * (1.0 / 4096) + 1e-05)
-        sc[rows, :] = jnp.broadcast_to(s, (16, 128))
         n = (x * s).astype(BF16)
         for yy in range(4):
             for b in range(4):
@@ -144,6 +168,16 @@
     remote(half(vg_hbm, 0, 1), half(vgp, 3, 1), VG + 1, ypeer(3)).wait_recv()
     go(remote(half(vgp, 3, 1), half(vgp, 2, 1), VG + 5, ypeer(3)))
 
+    @pl.when(z == 2)
+    def _():
+        from_left(1, 0)
+        wright(1, 0).start()
+
+    @pl.when(z == 1)
+    def _():
+        from_right(1, 0)
+        wleft(1, 0).start()
+
     upper = z // 2
     near = z + upper * (3 - 2 * z)
 
@@ -170,48 +204,25 @@
 
     lax.fori_loop(0, ROWS // 64, own_rows, 0)
 
-    def weights_arrive(s):
-        @pl.when(z - s >= 0)
-        def _():
-            remote(wp.at[z - s], wp.at[z - s], WL + s - 1, dev(y, z)).wait_recv()
-
-            @pl.when(z < 3)
-            def _():
-                wright(s).start()
-
-        @pl.when(z + s <= 3)
-        def _():
-            remote(wp.at[z + s], wp.at[z + s], WR + s - 1, dev(y, z)).wait_recv()
-
-            @pl.when(z > 0)
-            def _():
-                wleft(s).start()
-
-        if s >= 2:
-            @pl.when(z == 3)
-            def _():
-                far(3 - s).start()
-
-            @pl.when(z == 0)
-            def _():
-                far(s).start()
-
-    def rsright(b):
-        return remote(rsend.at[b], rr.at[b], RR + b, dev(y, z + 1))
-
-    def rsleft(b):
-        return remote(rsend.at[b], rl.at[b], RL + b, dev(y, z - 1))
-
-    def round_block(b, other=None):
+    def half_rows(h):
+        return pl.ds(h * 128, 128)
+
+    def rsright(b, h):
+        return remote(rsend.at[b, half_rows(h)], rr.at[b, half_rows(h)], RR + 2 * b + h, dev(y, z + 1))
+
+    def rsleft(b, h):
+        return remote(rsend.at[b, half_rows(h)], rl.at[b, half_rows(h)], RL + 2 * b + h, dev(y, z - 1))
+
+    def round_half(b, h, other=None):
         def rows_body(i, carry):
-            rows = pl.ds(pl.multiple_of(i * 32, 32), 32)
+            rows = pl.ds(pl.multiple_of(h * 128 + i * 32, 32), 32)
             g = gbuf[b, rows, :]
             if other is not None:
                 g = g + other[b, rows, :].astype(F32)
             rsend[b, rows, :] = g.astype(BF16)
             return carry
 
-        lax.fori_loop(0, BLK // 32, rows_body, 0)
+        lax.fori_loop(0, 4, rows_body, 0)
 
     def weight_grad(i):
         b = order(i)
@@ -228,17 +239,23 @@
         if i < 3:
             @pl.when(z == 0)
             def _():
-                round_block(3 - i)
-                rsright(3 - i).start()
+                for h in (0, 1):
+                    round_half(3 - i, h)
+                    rsright(3 - i, h).start()
 
             @pl.when(z == 3)
             def _():
-                round_block(i)
-                rsleft(i).start()
+                for h in (0, 1):
+                    round_half(i, h)
+                    rsleft(i, h).start()
 
     def ucopy(i, r):
         b = order(i)
         return remote(us.at[b, slot(r)], ur.at[y, b], US + 3 * i + r - 1, ypeer(4 - r))
+
+    def own_ur(i):
+        b = order(i)
+        return pltpu.make_async_copy(us.at[b, slot(0)], ur.at[y, b], osem.at[3 + i])
 
     def unit_grad(i):
         b = order(i)
@@ -256,41 +273,110 @@
         gg[b] = lax.fori_loop(0, 4, tokens, jnp.zeros((8, BLK), F32))
         for r in (1, 3, 2):
             go(ucopy(i, r))
-        ur[y, b] = us[b, 0:ROWS, :]
-
-    weights_arrive(1)
+        own_ur(i).start()
+
+    def relay_right(s):
+        for h in (0, 1):
+            from_left(s, h)
+            wright(s, h).start()
+
+    def relay_left(s):
+        for h in (0, 1):
+            from_right(s, h)
+            wleft(s, h).start()
+
+    @pl.when(z == 2)
+    def _():
+        from_left(1, 1)
+        wright(1, 1).start()
+        wright(0, 1).start()
+        relay_left(1)
+
+    @pl.when(z == 1)
+    def _():
+        from_right(1, 1)
+        wleft(1, 1).start()
+        wleft(0, 1).start()
+        relay_right(1)
+
+    def gossip_out(s, h):
+        @pl.when(z == 3)
+        def _():
+            from_left(s, h)
+            far(3 - s, h).start()
+
+        @pl.when(z == 0)
+        def _():
+            from_right(s, h)
+            far(s, h).start()
+
+    def forward_right(b, h):
+        remote(rsend.at[b, half_rows(h)], rr.at[b, half_rows(h)], RR + 2 * b + h, dev(y, z)).wait_recv()
+        round_half(b, h, rr)
+        rsright(b, h).start()
+
+    def forward_left(b, h):
+        remote(rsend.at[b, half_rows(h)], rl.at[b, half_rows(h)], RL + 2 * b + h, dev(y, z)).wait_recv()
+        round_half(b, h, rl)
+        rsleft(b, h).start()
+
+    def forward_first(h):
+        @pl.when(z == 1)
+        def _():
+            forward_right(3, h)
+
+        @pl.when(z == 2)
+        def _():
+            forward_left(0, h)
+
+    def forward_second(h):
+        @pl.when(z == 1)
+        def _():
+            forward_left(0, h)
+            forward_right(2, h)
+
+        @pl.when(z == 2)
+        def _():
+            forward_right(3, h)
+            forward_left(1, h)
+
+    gossip_out(2, 0)
     loads[2].wait()
     for k, (s, h) in ((4, (2, 0)), (5, (2, 1)), (2, (1, 1)), (3, (3, 0))):
         remote(half(vgp, s, h), half(vgp, s, h), VG + k, ypeer(1)).wait_recv()
+    gossip_out(2, 1)
     weight_grad(0)
-    weights_arrive(2)
+
+    @pl.when(z == 2)
+    def _():
+        relay_right(2)
+
+    @pl.when(z == 1)
+    def _():
+        relay_left(2)
+
     weight_grad(1)
+    forward_first(0)
     weight_grad(2)
-    weights_arrive(3)
-
-    def forward_right(b):
-        remote(rsend.at[b], rr.at[b], RR + b, dev(y, z)).wait_recv()
-        round_block(b, rr)
-        rsright(b).start()
-
-    def forward_left(b):
-        remote(rsend.at[b], rl.at[b], RL + b, dev(y, z)).wait_recv()
-        round_block(b, rl)
-        rsleft(b).start()
+    gossip_out(3, 0)
+    gossip_out(3, 1)
+
+    @pl.when(z == 3)
+    def _():
+        from_left(1, 0)
+        from_left(1, 1)
+
+    @pl.when(z == 0)
+    def _():
+        from_right(1, 0)
+        from_right(1, 1)
 
     unit_grad(0)
+    forward_first(1)
     unit_grad(1)
-
-    @pl.when(z == 1)
-    def _():
-        forward_right(3)
-
-    @pl.when(z == 2)
-    def _():
-        forward_left(0)
-
     unit_grad(2)
     weight_grad(3)
+    forward_second(0)
     unit_grad(3)
 
     def ggcopy(d):
@@ -300,15 +386,7 @@
     for d in (1, 2, 3):
         go(ggcopy(d))
 
-    @pl.when(z == 1)
-    def _():
-        forward_right(2)
-        forward_left(0)
-
-    @pl.when(z == 2)
-    def _():
-        forward_left(1)
-        forward_right(3)
+    forward_second(1)
 
     total = (mix[0, 0, 0] + mix[0, 0, 1] + mix[0, 0, 2] + mix[0, 0, 3] + mix[0, 0, 4]).astype(F32)
 
@@ -331,7 +409,10 @@
     remote(gos.at[2], gos.at[2], GO + 2, dev(y, z)).wait_recv()
     remote(gos.at[0], gos.at[0], GO + 0, dev(y, z)).wait_recv()
     remote(gos.at[1], gos.at[1], GO + 1, dev(y, z)).wait_recv()
-    remote(gos.at[3], gos.at[3], GO + 3, dev(y, z)).wait_recv()
+    far_in = gos.at[3, pl.ds(0, 128)]
+    remote(far_in, far_in, GO + 3, dev(y, z)).wait_recv()
+    far_in = gos.at[3, pl.ds(128, 144)]
+    remote(far_in, far_in, GO + 4, dev(y, z)).wait_recv()
 
     def gossip_gain(n):
         return gos[n, BLK:WROWS, 0:BLK].astype(F32)[0:1, :]
@@ -345,23 +426,13 @@
     col = jnp.sum(jnp.where(eye, jnp.broadcast_to(gain_row.astype(F32), (BLK, BLK)), 0.0), axis=1, keepdims=True)
     gcol[...] = jnp.broadcast_to(col, (BLK, 128))
 
-    def add_block(other):
-        def rows_body(i, carry):
-            rows = pl.ds(pl.multiple_of(i * 32, 32), 32)
-            gbuf[z, rows, :] = gbuf[z, rows, :] + other[z, rows, :].astype(F32)
-            return carry
-
-        lax.fori_loop(0, BLK // 32, rows_body, 0)
-
-    @pl.when(z > 0)
-    def _():
-        remote(rsend.at[z], rr.at[z], RR + z, dev(y, z)).wait_recv()
-        add_block(rr)
-
-    @pl.when(z < 3)
-    def _():
-        remote(rsend.at[z], rl.at[z], RL + z, dev(y, z)).wait_recv()
-        add_block(rl)
+    @pl.when(z == 0)
+    def _():
+        rr[z] = jnp.zeros((BLK, KV), BF16)
+
+    @pl.when(z == 3)
+    def _():
+        rl[z] = jnp.zeros((BLK, KV), BF16)
 
     loads[3].wait()
     loads[4].wait()
@@ -370,89 +441,119 @@
 
     def adam_rows(i, carry):
         rows = pl.ds(pl.multiple_of(i * 16, 16), 16)
-        g = gcol[rows, 0:1] * gbuf[z, rows, :]
+        g = gbuf[z, rows, :] + rr[z, rows, :].astype(F32) + rl[z, rows, :].astype(F32)
+        g = gcol[rows, 0:1] * g
         new_m = 0.9 * mv[rows, :] + 0.1 * g
         new_v = 0.999 * vv[rows, :] + 0.001 * g * g
-        nm[rows, :] = new_m
-        nv[rows, :] = new_v
+        mv[rows, :] = new_m
+        vv[rows, :] = new_v
         own = wf[rows, :]
         stepped = own - 0.01 * (new_m / (jnp.sqrt(new_v) + 1e-08) + 0.1 * own)
         out = s0 * stepped + s1 * gos[0, rows, :].astype(F32) + s2 * gos[1, rows, :].astype(F32)
-        nw[rows, :] = out + s3 * gos[2, rows, :].astype(F32) + s4 * gos[3, rows, :].astype(F32)
+        wf[rows, :] = out + s3 * gos[2, rows, :].astype(F32) + s4 * gos[3, rows, :].astype(F32)
         return carry
 
-    lax.fori_loop(0, BLK // 16, adam_rows, 0)
+    for h in (0, 1):
+        @pl.when(z > 0)
+        def _():
+            remote(rsend.at[z, half_rows(h)], rr.at[z, half_rows(h)], RR + 2 * z + h, dev(y, z)).wait_recv()
+
+        @pl.when(z < 3)
+        def _():
+            remote(rsend.at[z, half_rows(h)], rl.at[z, half_rows(h)], RL + 2 * z + h, dev(y, z)).wait_recv()
+
+        lax.fori_loop(8 * h, 8 * h + 8, adam_rows, 0)
+
+    writes = [
+        pltpu.make_async_copy(wf, nw, osem.at[0]),
+        pltpu.make_async_copy(mv, nm, osem.at[1]),
+        pltpu.make_async_copy(vv, nv, osem.at[2]),
+    ]
+    for c in writes:
+        c.start()
 
     for i in range(4):
         for r in (1, 3, 2):
             ucopy(i, r).wait_recv()
+        own_ur(i).wait()
+    for c in writes:
+        c.wait()
+
+    for _, copy in sent:
+        copy.wait_send()
+    for h in (0, 1):
+        for s, right, left in (
+            (0, z < 3, z > 0),
+            (1, (z == 1) | (z == 2), (z == 1) | (z == 2)),
+            (2, z == 2, z == 1),
+        ):
+            @pl.when(right)
+            def _():
+                wright(s, h).wait_send()
+
+            @pl.when(left)
+            def _():
+                wleft(s, h).wait_send()
+
+        for s in (2, 3):
+            @pl.when(z == 3)
+            def _():
+                far(3 - s, h).wait_send()
+
+            @pl.when(z == 0)
+            def _():
+                far(s, h).wait_send()
+
+        for b in range(4):
+            @pl.when(z < b)
+            def _():
+                rsright(b, h).wait_send()
+
+            @pl.when(z > b)
+            def _():
+                rsleft(b, h).wait_send()
+
+
+def finish_kernel(x, ur, nw, nm, nv, ng, ngm, ngv, ig, nw_out, nm_out, nv_out, ng_out, ngm_out, ngv_out):
+    nw_out[...] = nw[...]
+    nm_out[...] = nm[...]
+    nv_out[...] = nv[...]
+    ng_out[...] = ng[...]
+    ngm_out[...] = ngm[...]
+    ngv_out[...] = ngv[...]
 
     def grad_rows(i, carry):
         rows = pl.ds(pl.multiple_of(i * 16, 16), 16)
-        s = sc[rows, 0:1]
-        inner = jnp.zeros((16, 1), F32)
+        own = x[rows, :].astype(F32)
+        s = lax.rsqrt(jnp.sum(own * own, axis=1, keepdims=True) * (1.0 / 4096) + 1e-05)
+        inner = jnp.zeros((16, BLK), F32)
         for yy in range(4):
             for b in range(4):
                 at = yy * WIDE + b * BLK
-                unit = xv[rows, at:at + BLK].astype(F32) * s
-                inner = inner + jnp.sum(ur[yy, b, rows, :].astype(F32) * unit, axis=1, keepdims=True)
-        inner = inner * (1.0 / 4096)
+                inner = inner + ur[yy, b, rows, :].astype(F32) * (own[:, at:at + BLK] * s)
+        inner = jnp.sum(inner, axis=1, keepdims=True) * (1.0 / 4096)
         for yy in range(4):
             for b in range(4):
                 at = yy * WIDE + b * BLK
-                unit = xv[rows, at:at + BLK].astype(F32) * s
+                unit = own[:, at:at + BLK] * s
                 ig[rows, at:at + BLK] = s * (ur[yy, b, rows, :].astype(F32) - unit * inner)
         return carry
 
-    lax.fori_loop(0, ROWS // 16, grad_rows, 0)
-
-    for _, copy in sent:
-        copy.wait_send()
-    for s in range(3):
-        @pl.when((z < 3) & (z - s >= 0))
-        def _():
-            wright(s).wait_send()
-
-        @pl.when((z > 0) & (z + s <= 3))
-        def _():
-            wleft(s).wait_send()
-
-    for s in (2, 3):
-        @pl.when(z == 3)
-        def _():
-            far(3 - s).wait_send()
-
-        @pl.when(z == 0)
-        def _():
-            far(s).wait_send()
-
-    for b in range(4):
-        @pl.when(z < b)
-        def _():
-            rsright(b).wait_send()
-
-        @pl.when(z > b)
-        def _():
-            rsleft(b).wait_send()
+    lax.fori_loop(0, x.shape[0] // 16, grad_rows, 0)
 
 
 def body(inputs, value_grad, weight, weight_m, weight_v, gain, gain_m, gain_v, mixing):
     vmem = pl.BlockSpec(memory_space=pltpu.VMEM)
     hbm = pl.BlockSpec(memory_space=pl.ANY)
-    outs = pl.pallas_call(
+    tokens = inputs.reshape(ROWS, 4 * WIDE)
+    weights = [jax.ShapeDtypeStruct((BLK, KV), F32)] * 3
+    gains = [jax.ShapeDtypeStruct((1, 1, BLK), F32)] * 3
+    parts = pl.pallas_call(
         step_kernel,
         name="gossip_step",
-        out_shape=[
-            jax.ShapeDtypeStruct((ROWS, 4 * WIDE), F32),
-            jax.ShapeDtypeStruct((BLK, KV), F32),
-            jax.ShapeDtypeStruct((BLK, KV), F32),
-            jax.ShapeDtypeStruct((BLK, KV), F32),
-            jax.ShapeDtypeStruct((1, 1, BLK), F32),
-            jax.ShapeDtypeStruct((1, 1, BLK), F32),
-            jax.ShapeDtypeStruct((1, 1, BLK), F32),
-        ],
+        out_shape=[jax.ShapeDtypeStruct((4, 4, ROWS, BLK), BF16)] + weights + gains,
         in_specs=[pl.BlockSpec(memory_space=pltpu.SMEM)] + [hbm] * 5 + [vmem] * 3,
-        out_specs=[vmem] * 7,
+        out_specs=[hbm] * 4 + [vmem] * 3,
         scratch_shapes=[
             pltpu.VMEM((ROWS, 4 * WIDE), BF16),
             pltpu.VMEM((BLK, KV), F32),
@@ -464,7 +565,6 @@
             pltpu.VMEM((BLK, 4 * ROWS), BF16),
             pltpu.VMEM((4, WROWS, KV), BF16),
             pltpu.VMEM((4, 4 * ROWS, BLK), BF16),
-            pltpu.VMEM((4, 4, ROWS, BLK), BF16),
             pltpu.VMEM((4, BLK, KV), F32),
             pltpu.VMEM((4, BLK, KV), BF16),
             pltpu.VMEM((4, BLK, KV), BF16),
@@ -472,18 +572,18 @@
             pltpu.VMEM((4, 8, BLK), F32),
             pltpu.VMEM((3, 8, BLK), F32),
             pltpu.VMEM((4, WROWS, KV), BF16),
-            pltpu.VMEM((ROWS, 128), F32),
             pltpu.VMEM((BLK, 128), F32),
             pltpu.SemaphoreType.DMA((5,)),
+            pltpu.SemaphoreType.DMA((7,)),
             pltpu.SemaphoreType.DMA((NSEM,)),
             pltpu.SemaphoreType.DMA((NSEM,)),
         ],
         compiler_params=pltpu.CompilerParams(
-            collective_id=0, has_side_effects=True, vmem_limit_bytes=56 << 20
+            collective_id=0, has_side_effects=True, vmem_limit_bytes=60 << 20
         ),
     )(
         mixing,
-        inputs.reshape(ROWS, 4 * WIDE),
+        tokens,
         value_grad.reshape(ROWS, KV),
         weight[0, 0],
         weight_m[0, 0],
@@ -492,7 +592,20 @@
         gain_m,
         gain_v,
     )
-    ig, nw, nm, nv, ng, ngm, ngv = outs
+    steps = 4
+    wide_block = pl.BlockSpec((ROWS // steps, 4 * WIDE), lambda i: (i, 0))
+    row_block = pl.BlockSpec((BLK // steps, KV), lambda i: (i, 0))
+    gain_block = pl.BlockSpec((1, 1, BLK), lambda i: (0, 0, 0))
+    ig, nw, nm, nv, ng, ngm, ngv = pl.pallas_call(
+        finish_kernel,
+        name="finish",
+        grid=(steps,),
+        out_shape=[jax.ShapeDtypeStruct((ROWS, 4 * WIDE), F32)] + weights + gains,
+        in_specs=[wide_block, pl.BlockSpec((4, 4, ROWS // steps, BLK), lambda i: (0, 0, i, 0))]
+        + [row_block] * 3 + [gain_block] * 3,
+        out_specs=[wide_block] + [row_block] * 3 + [gain_block] * 3,
+        compiler_params=pltpu.CompilerParams(vmem_limit_bytes=60 << 20),
+    )(tokens, *parts)
     return (ig.reshape(inputs.shape), nw[None, None], nm[None, None], nv[None, None], ng, ngm, ngv)
 
 

time: 106 us -> 89.3 us (0.84)
  local copies, waits for them, and re-layouts: 9.42 us -> 0 us
  Pallas kernels: 96.1 us -> 88.5 us
    pallas_call x1, Pallas kernels: 96.1 us -> 80.3 us  [body(): pl.pallas_call(step_kernel, name='gossip_step', out_shape=[jax.ShapeDtype...]
    unnamed x19 -> x0, local copies, waits for them, and re-layouts: 9.42 us -> none
    pallas_call x0 -> x1, Pallas kernels: none -> 8.26 us  [body(): pl.pallas_call(finish_kernel, name='finish', grid=(steps,), out_shape=[ja...]
where the time goes in v2:
time: 89.3 us; the launch traced here: 89.2 us
  Pallas kernels  88.5 us (99%)
    pallas_call x1, Pallas kernels, body(): pl.pallas_call(step_kernel, name='gossip_step', out_shape=[jax.ShapeDtype...  80.3 us
    pallas_call x1, Pallas kernels, body(): pl.pallas_call(finish_kernel, name='finish', grid=(steps,), out_shape=[ja...  8.26 us

profile of v2, /device:TPU:1, one launch (start us, length us, event | category | flops | bytes accessed | tf_op | source)
XLA Modules:
  0.0 89.2 jit_solution(10583766429614207555)
XLA Ops:
  0.6 80.3 %gossip_step.1 = (bf16[4,4,256,256]{3,2,1,0:T(8,128)(2,1)}, f32[256,1024]{1,0:T(8,128)}, f32[256,1024]{1,0:T(8,128)}, f32[256,1024]{1,0:T(8,128)}, f32[1,1,256]{...) custom-call(s32[1,1,5]{2,1,0:T(1,128)} %mix.1, bf16[256,4096]{1,0:T(8,128)(2,1)} %bitcast.9, ...), custom_call_target="tpu_custom_call" | custom-call | tf_op jit(solution)/shard_map/gossip_step/pallas_call | solution.py:551
  80.9 8.3 %finish.1 = (f32[256,4096]{1,0:T(8,128)}, f32[256,1024]{1,0:T(8,128)}, f32[256,1024]{1,0:T(8,128)}, f32[256,1024]{1,0:T(8,128)}, f32[1,1,256]{2,1,0:T(1,128)}, /...) custom-call(bf16[256,4096]{1,0:T(8,128)(2,1)} %bitcast.10, bf16[4,4,256,256]{3,2,1,0:T(8,128)(2,1)} %get-tuple-element.21.ur, ...), custom_call_target="tpu_custom_call" | custom-call | tf_op jit(solution)/shard_map/finish/pallas_call | solution.py:599

commit v3 on v2

--- a/solution.py
+++ b/solution.py
@@ -33,12 +33,28 @@
             return c
 
 
+def mirrored(z, codes, i):
+    upper = z // 2
+    near = z + upper * (3 - 2 * z)
+    t = ((codes[0] + (codes[1] - codes[0]) * near) // 4**i) % 4
+    return t + upper * (3 - 2 * t)
+
+
+def grad_order(z, i):
+    return mirrored(z, (27, 99), i)
+
+
+def unit_order(z, i):
+    return mirrored(z, (216, 225), i)
+
+
 def step_kernel(
     mix, x_hbm, vg_hbm, w_hbm, m_hbm, v_hbm, gain, gain_m, gain_v,
-    ur, nw, nm, nv, ng, ngm, ngv,
-    xv, wf, mv, vv, vgp, nown, npool, npt, wp, us, gbuf, rsend, rr, rl, gg, ggr, gos, gcol,
-    lsem, osem, ssem, rsem,
+    ur0, ur1, ur2, ur3, xv, sc, acc, nw, nm, nv, ng, ngm, ngv,
+    wf, mv, vv, vgp, nown, npool, npt, wp, us, gbuf, rsend, rr, rl, gg, ggr, gos, gcol,
+    lsem, ssem, rsem,
 ):
+    ur = (ur0, ur1, ur2, ur3)
     rx = lax.axis_index("rx")
     ry = lax.axis_index("ry")
     f = lax.axis_index("fsdp")
@@ -62,6 +78,14 @@
             device_id=device, device_id_type=MESH,
         )
 
+    barrier = pltpu.get_barrier_semaphore()
+    far_base = (1 - z // 2) * 2
+    partners = [ypeer(1), ypeer(2), ypeer(3)]
+    partners += [dev(y, (z + 1) % 4), dev(y, (z + 2) % 4), dev(y, (z + 3) % 4)]
+    partners += [(rx, (ry + 1) % 4, f), (rx, (ry + 3) % 4, f), (chip_rx, ry, f)]
+    partners += [(far_rx, ry, y * 4 + far_base), (far_rx, ry, y * 4 + far_base + 1)]
+    for p in partners:
+        pl.semaphore_signal(barrier, inc=1, device_id=p, device_id_type=MESH)
     loads = [
         pltpu.make_async_copy(w_hbm, wf, lsem.at[0]),
         pltpu.make_async_copy(x_hbm, xv, lsem.at[1]),
@@ -72,14 +96,6 @@
     for c in loads:
         c.start()
 
-    barrier = pltpu.get_barrier_semaphore()
-    far_base = (1 - z // 2) * 2
-    partners = [ypeer(1), ypeer(2), ypeer(3)]
-    partners += [dev(y, (z + 1) % 4), dev(y, (z + 2) % 4), dev(y, (z + 3) % 4)]
-    partners += [(rx, (ry + 1) % 4, f), (rx, (ry + 3) % 4, f), (chip_rx, ry, f)]
-    partners += [(far_rx, ry, y * 4 + far_base), (far_rx, ry, y * 4 + far_base + 1)]
-    for p in partners:
-        pl.semaphore_signal(barrier, inc=1, device_id=p, device_id_type=MESH)
     pl.semaphore_wait(barrier, len(partners))
 
     sent = []
@@ -151,17 +167,22 @@
     loads[1].wait()
 
     def norm_rows(i, carry):
-        rows = pl.ds(pl.multiple_of(i * 16, 16), 16)
-        x = xv[rows, :].astype(F32)
-        s = lax.rsqrt(jnp.sum(x * x, axis=1, keepdims=True) * (1.0 / 4096) + 1e-05)
-        n = (x * s).astype(BF16)
+        rows = pl.ds(pl.multiple_of(i * 64, 64), 64)
+        part = jnp.zeros((64, 128), F32)
+        for c in range(4 * WIDE // 128):
+            x = xv[rows, c * 128:(c + 1) * 128].astype(F32)
+            part = part + x * x
+        s = lax.rsqrt(jnp.sum(part, axis=1, keepdims=True) * (1.0 / 4096) + 1e-05)
+        s = jnp.broadcast_to(s, (64, 128))
+        sc[rows, :] = s
         for yy in range(4):
             for b in range(4):
-                at = yy * WIDE + b * BLK
-                nown[yy, b, rows, :] = n[:, at:at + BLK]
+                for c in (0, 128):
+                    at = yy * WIDE + b * BLK + c
+                    nown[yy, b, rows, c:c + 128] = (xv[rows, at:at + 128].astype(F32) * s).astype(BF16)
         return carry
 
-    lax.fori_loop(0, ROWS // 16, norm_rows, 0)
+    lax.fori_loop(0, ROWS // 64, norm_rows, 0)
 
     remote(half(vg_hbm, 0, 0), half(vgp, 1, 0), VG + 0, ypeer(1)).wait_recv()
     go(remote(half(vgp, 1, 0), half(vgp, 2, 0), VG + 4, ypeer(1)))
@@ -178,12 +199,8 @@
         from_right(1, 0)
         wleft(1, 0).start()
 
-    upper = z // 2
-    near = z + upper * (3 - 2 * z)
-
     def order(i):
-        t = ((27 + 72 * near) // 4**i) % 4
-        return t + upper * (3 - 2 * t)
+        return grad_order(z, i)
 
     def slot(r):
         return pl.ds(r * ROWS, ROWS)
@@ -250,30 +267,42 @@
                     rsleft(i, h).start()
 
     def ucopy(i, r):
-        b = order(i)
-        return remote(us.at[b, slot(r)], ur.at[y, b], US + 3 * i + r - 1, ypeer(4 - r))
-
-    def own_ur(i):
-        b = order(i)
-        return pltpu.make_async_copy(us.at[b, slot(0)], ur.at[y, b], osem.at[3 + i])
+        b = unit_order(z, i)
+        return remote(us.at[b, slot(r)], ur[i].at[y], US + 3 * i + r - 1, ypeer(4 - r))
 
     def unit_grad(i):
-        b = order(i)
+        b = unit_order(z, i)
         gl = wp[b, BLK:WROWS, 0:BLK].astype(F32)[0:1, :]
 
-        def tokens(r, acc):
+        def tokens(r, carry):
             rows = pl.ds(pl.multiple_of(r * ROWS, ROWS), ROWS)
             og = lax.dot_general(
                 vgp[rows, :], wp[b, 0:BLK, :], (((1,), (1,)), ((), ())), preferred_element_type=F32
             )
             us[b, rows, :] = (og * gl).astype(BF16)
-            prod = og * npool[b, rows, :].astype(F32)
-            return acc + jnp.sum(prod.reshape(ROWS // 8, 8, BLK), axis=0)
-
-        gg[b] = lax.fori_loop(0, 4, tokens, jnp.zeros((8, BLK), F32))
+            return carry
+
+        lax.fori_loop(0, 4, tokens, 0)
         for r in (1, 3, 2):
             go(ucopy(i, r))
-        own_ur(i).start()
+        ur[i][y] = us[b, 0:ROWS, :]
+
+    eye = lax.broadcasted_iota(jnp.int32, (BLK, BLK), 0) == lax.broadcasted_iota(jnp.int32, (BLK, BLK), 1)
+
+    def gain_grad(b):
+        def rows_body(i, carry):
+            rows = pl.ds(pl.multiple_of(i * 64, 64), 64)
+            part = jnp.zeros((64, 128), F32)
+            for c in range(KV // 128):
+                cols = pl.ds(c * 128, 128)
+                part = part + wp[b, rows, cols].astype(F32) * gbuf[b, rows, cols]
+            gcol[rows, :] = part
+            return carry
+
+        lax.fori_loop(0, BLK // 64, rows_body, 0)
+        col = jnp.sum(gcol[...], axis=1, keepdims=True)
+        spread = jnp.where(eye, jnp.broadcast_to(col, (BLK, BLK)), 0.0)
+        gg[b] = jnp.sum(spread.reshape(BLK // 8, 8, BLK), axis=0)
 
     def relay_right(s):
         for h in (0, 1):
@@ -345,6 +374,7 @@
     for k, (s, h) in ((4, (2, 0)), (5, (2, 1)), (2, (1, 1)), (3, (3, 0))):
         remote(half(vgp, s, h), half(vgp, s, h), VG + k, ypeer(1)).wait_recv()
     gossip_out(2, 1)
+    unit_grad(0)
     weight_grad(0)
 
     @pl.when(z == 2)
@@ -355,29 +385,34 @@
     def _():
         relay_left(2)
 
+    unit_grad(1)
     weight_grad(1)
     forward_first(0)
+
+    @pl.when(z == 3)
+    def _():
+        from_left(1, 0)
+        from_left(1, 1)
+
+    @pl.when(z == 0)
+    def _():
+        from_right(1, 0)
+        from_right(1, 1)
+
+    unit_grad(2)
     weight_grad(2)
     gossip_out(3, 0)
     gossip_out(3, 1)
-
-    @pl.when(z == 3)
-    def _():
-        from_left(1, 0)
-        from_left(1, 1)
-
-    @pl.when(z == 0)
-    def _():
-        from_right(1, 0)
-        from_right(1, 1)
-
-    unit_grad(0)
     forward_first(1)
-    unit_grad(1)
-    unit_grad(2)
+    unit_grad(3)
     weight_grad(3)
     forward_second(0)
-    unit_grad(3)
+
+    def gain_block(b, carry):
+        gain_grad(b)
+        return carry
+
+    lax.fori_loop(0, 4, gain_block, 0)
 
     def ggcopy(d):
         zz = (z + d) % 4
@@ -422,7 +457,6 @@
     mixed_g = mixed_g + share(from_chip, BLK) * gossip_gain(2) + share(from_far, BLK) * gossip_gain(3)
     ng[0] = mixed_g
 
-    eye = lax.broadcasted_iota(jnp.int32, (BLK, BLK), 0) == lax.broadcasted_iota(jnp.int32, (BLK, BLK), 1)
     col = jnp.sum(jnp.where(eye, jnp.broadcast_to(gain_row.astype(F32), (BLK, BLK)), 0.0), axis=1, keepdims=True)
     gcol[...] = jnp.broadcast_to(col, (BLK, 128))
 
@@ -440,44 +474,50 @@
     s3, s4 = share(from_chip, KV), share(from_far, KV)
 
     def adam_rows(i, carry):
-        rows = pl.ds(pl.multiple_of(i * 16, 16), 16)
+        rows = pl.ds(pl.multiple_of(i * 32, 32), 32)
         g = gbuf[z, rows, :] + rr[z, rows, :].astype(F32) + rl[z, rows, :].astype(F32)
         g = gcol[rows, 0:1] * g
         new_m = 0.9 * mv[rows, :] + 0.1 * g
         new_v = 0.999 * vv[rows, :] + 0.001 * g * g
-        mv[rows, :] = new_m
-        vv[rows, :] = new_v
+        nm[rows, :] = new_m
+        nv[rows, :] = new_v
         own = wf[rows, :]
         stepped = own - 0.01 * (new_m / (jnp.sqrt(new_v) + 1e-08) + 0.1 * own)
         out = s0 * stepped + s1 * gos[0, rows, :].astype(F32) + s2 * gos[1, rows, :].astype(F32)
-        wf[rows, :] = out + s3 * gos[2, rows, :].astype(F32) + s4 * gos[3, rows, :].astype(F32)
+        nw[rows, :] = out + s3 * gos[2, rows, :].astype(F32) + s4 * gos[3, rows, :].astype(F32)
         return carry
 
-    for h in (0, 1):
-        @pl.when(z > 0)
-        def _():
-            remote(rsend.at[z, half_rows(h)], rr.at[z, half_rows(h)], RR + 2 * z + h, dev(y, z)).wait_recv()
-
-        @pl.when(z < 3)
-        def _():
-            remote(rsend.at[z, half_rows(h)], rl.at[z, half_rows(h)], RL + 2 * z + h, dev(y, z)).wait_recv()
-
-        lax.fori_loop(8 * h, 8 * h + 8, adam_rows, 0)
-
-    writes = [
-        pltpu.make_async_copy(wf, nw, osem.at[0]),
-        pltpu.make_async_copy(mv, nm, osem.at[1]),
-        pltpu.make_async_copy(vv, nv, osem.at[2]),
-    ]
-    for c in writes:
-        c.start()
-
-    for i in range(4):
+    def add_inner(i):
         for r in (1, 3, 2):
             ucopy(i, r).wait_recv()
-        own_ur(i).wait()
-    for c in writes:
-        c.wait()
+        ats = [pl.multiple_of(yy * WIDE + unit_order(z, i) * BLK, BLK) for yy in range(4)]
+
+        def rows_body(k, carry):
+            rows = pl.ds(pl.multiple_of(k * 64, 64), 64)
+            part = jnp.zeros((64, BLK), F32) if i == 0 else acc[rows, :]
+            for yy in range(4):
+                x = xv[rows, pl.ds(ats[yy], BLK)].astype(F32)
+                part = part + ur[i][yy, rows, :].astype(F32) * x
+            acc[rows, :] = part
+            return carry
+
+        lax.fori_loop(0, ROWS // 64, rows_body, 0)
+
+    for h in (0, 1):
+        add_inner(h)
+
+        @pl.when(z > 0)
+        def _():
+            remote(rsend.at[z, half_rows(h)], rr.at[z, half_rows(h)], RR + 2 * z + h, dev(y, z)).wait_recv()
+
+        @pl.when(z < 3)
+        def _():
+            remote(rsend.at[z, half_rows(h)], rl.at[z, half_rows(h)], RL + 2 * z + h, dev(y, z)).wait_recv()
+
+        lax.fori_loop(4 * h, 4 * h + 4, adam_rows, 0)
+
+    add_inner(2)
+    add_inner(3)
 
     for _, copy in sent:
         copy.wait_send()
@@ -514,48 +554,64 @@
                 rsleft(b, h).wait_send()
 
 
-def finish_kernel(x, ur, nw, nm, nv, ng, ngm, ngv, ig, nw_out, nm_out, nv_out, ng_out, ngm_out, ngv_out):
-    nw_out[...] = nw[...]
-    nm_out[...] = nm[...]
-    nv_out[...] = nv[...]
+def finish_kernel(
+    ur0, ur1, ur2, ur3, x, sc, acc, nw, nm, nv, ng, ngm, ngv,
+    ig, nw_out, nm_out, nv_out, ng_out, ngm_out, ngv_out,
+    grad, sem, grad_sem,
+):
+    writes = [
+        pltpu.make_async_copy(nw, nw_out, sem.at[0]),
+        pltpu.make_async_copy(nm, nm_out, sem.at[1]),
+        pltpu.make_async_copy(nv, nv_out, sem.at[2]),
+    ]
+    for c in writes:
+        c.start()
     ng_out[...] = ng[...]
     ngm_out[...] = ngm[...]
     ngv_out[...] = ngv[...]
 
+    z = lax.axis_index("fsdp") % 4
+    blocks = []
+    for i, ref in enumerate((ur0, ur1, ur2, ur3)):
+        for yy in range(4):
+            at = pl.multiple_of(yy * WIDE + unit_order(z, i) * BLK, BLK)
+            blocks.append((ref, yy, pl.ds(at, BLK)))
+
     def grad_rows(i, carry):
-        rows = pl.ds(pl.multiple_of(i * 16, 16), 16)
-        own = x[rows, :].astype(F32)
-        s = lax.rsqrt(jnp.sum(own * own, axis=1, keepdims=True) * (1.0 / 4096) + 1e-05)
-        inner = jnp.zeros((16, BLK), F32)
-        for yy in range(4):
-            for b in range(4):
-                at = yy * WIDE + b * BLK
-                inner = inner + ur[yy, b, rows, :].astype(F32) * (own[:, at:at + BLK] * s)
-        inner = jnp.sum(inner, axis=1, keepdims=True) * (1.0 / 4096)
-        for yy in range(4):
-            for b in range(4):
-                at = yy * WIDE + b * BLK
-                unit = own[:, at:at + BLK] * s
-                ig[rows, at:at + BLK] = s * (ur[yy, b, rows, :].astype(F32) - unit * inner)
+        rows = pl.ds(pl.multiple_of(i * 32, 32), 32)
+        s = sc[rows, :]
+        t = jnp.sum(acc[rows, :], axis=1, keepdims=True) * (1.0 / 4096)
+        t = jnp.broadcast_to(t, (32, 128)) * (s * s * s)
+        s, t = (jnp.concatenate([v, v], axis=1) for v in (s, t))
+        for ref, yy, cols in blocks:
+            grad[rows, cols] = s * ref[yy, rows, :].astype(F32) - x[rows, cols].astype(F32) * t
         return carry
 
-    lax.fori_loop(0, x.shape[0] // 16, grad_rows, 0)
+    parts = grad_sem.shape[0]
+    size = ROWS // parts
+    for p in range(parts):
+        lax.fori_loop(p * size // 32, (p + 1) * size // 32, grad_rows, 0)
+        rows = pl.ds(p * size, size)
+        c = pltpu.make_async_copy(grad.at[rows], ig.at[rows], grad_sem.at[p])
+        c.start()
+        writes.append(c)
+    for c in writes:
+        c.wait()
 
 
 def body(inputs, value_grad, weight, weight_m, weight_v, gain, gain_m, gain_v, mixing):
     vmem = pl.BlockSpec(memory_space=pltpu.VMEM)
     hbm = pl.BlockSpec(memory_space=pl.ANY)
     tokens = inputs.reshape(ROWS, 4 * WIDE)
-    weights = [jax.ShapeDtypeStruct((BLK, KV), F32)] * 3
-    gains = [jax.ShapeDtypeStruct((1, 1, BLK), F32)] * 3
+    shapes = [((ROWS, 4 * WIDE), F32)] + [((BLK, KV), F32)] * 3 + [((1, 1, BLK), F32)] * 3
+    passed = [((4, ROWS, BLK), BF16)] * 4 + [((ROWS, 4 * WIDE), BF16), ((ROWS, 128), F32), ((ROWS, BLK), F32)]
     parts = pl.pallas_call(
         step_kernel,
         name="gossip_step",
-        out_shape=[jax.ShapeDtypeStruct((4, 4, ROWS, BLK), BF16)] + weights + gains,
+        out_shape=[pltpu.VMEM(*a) for a in passed + shapes[1:]],
         in_specs=[pl.BlockSpec(memory_space=pltpu.SMEM)] + [hbm] * 5 + [vmem] * 3,
-        out_specs=[hbm] * 4 + [vmem] * 3,
+        out_specs=[vmem] * 13,
         scratch_shapes=[
-            pltpu.VMEM((ROWS, 4 * WIDE), BF16),
             pltpu.VMEM((BLK, KV), F32),
             pltpu.VMEM((BLK, KV), F32),
             pltpu.VMEM((BLK, KV), F32),
@@ -574,12 +630,11 @@
             pltpu.VMEM((4, WROWS, KV), BF16),
             pltpu.VMEM((BLK, 128), F32),
             pltpu.SemaphoreType.DMA((5,)),
-            pltpu.SemaphoreType.DMA((7,)),
             pltpu.SemaphoreType.DMA((NSEM,)),
             pltpu.SemaphoreType.DMA((NSEM,)),
         ],
         compiler_params=pltpu.CompilerParams(
-            collective_id=0, has_side_effects=True, vmem_limit_bytes=60 << 20
+            collective_id=0, has_side_effects=True, vmem_limit_bytes=50 << 20
         ),
     )(
         mixing,
@@ -592,20 +647,19 @@
         gain_m,
         gain_v,
     )
-    steps = 4
-    wide_block = pl.BlockSpec((ROWS // steps, 4 * WIDE), lambda i: (i, 0))
-    row_block = pl.BlockSpec((BLK // steps, KV), lambda i: (i, 0))
-    gain_block = pl.BlockSpec((1, 1, BLK), lambda i: (0, 0, 0))
     ig, nw, nm, nv, ng, ngm, ngv = pl.pallas_call(
         finish_kernel,
         name="finish",
-        grid=(steps,),
-        out_shape=[jax.ShapeDtypeStruct((ROWS, 4 * WIDE), F32)] + weights + gains,
-        in_specs=[wide_block, pl.BlockSpec((4, 4, ROWS // steps, BLK), lambda i: (0, 0, i, 0))]
-        + [row_block] * 3 + [gain_block] * 3,
-        out_specs=[wide_block] + [row_block] * 3 + [gain_block] * 3,
-        compiler_params=pltpu.CompilerParams(vmem_limit_bytes=60 << 20),
-    )(tokens, *parts)
+        out_shape=[jax.ShapeDtypeStruct(*a) for a in shapes],
+        in_specs=[vmem] * 13,
+        out_specs=[hbm] * 4 + [vmem] * 3,
+        scratch_shapes=[
+            pltpu.VMEM((ROWS, 4 * WIDE), F32),
+            pltpu.SemaphoreType.DMA((3,)),
+            pltpu.SemaphoreType.DMA((4,)),
+        ],
+        compiler_params=pltpu.CompilerParams(vmem_limit_bytes=16 << 20),
+    )(*parts)
     return (ig.reshape(inputs.shape), nw[None, None], nm[None, None], nv[None, None], ng, ngm, ngv)
 
 

time: 89.3 us -> 82.6 us (0.925)
  Pallas kernels: 88.5 us -> 81.9 us
    pallas_call x2, Pallas kernels: 88.5 us -> 81.9 us  [the longest x1 78.3 us: body(): pl.pallas_call(step_kernel, name='gossip_step', out_shape=[pltpu.VMEM(*a)...]
where the time goes in v3:
time: 82.6 us; the launch traced here: 82.5 us
  Pallas kernels  81.9 us (99%)
    pallas_call x1, Pallas kernels, body(): pl.pallas_call(step_kernel, name='gossip_step', out_shape=[pltpu.VMEM(*a)...  78.3 us
    pallas_call x1, Pallas kernels, body(): pl.pallas_call(finish_kernel, name='finish', out_shape=[jax.ShapeDtypeStr...  3.62 us

profile of v3, /device:TPU:1, one launch (start us, length us, event | category | flops | bytes accessed | tf_op | source)
XLA Modules:
  0.0 82.5 jit_solution(13249053367112490722)
XLA Ops:
  0.6 78.3 %gossip_step.1 = (bf16[4,256,256]{2,1,0:T(8,128)(2,1)S(1)}, bf16[4,256,256]{2,1,0:T(8,128)(2,1)S(1)}, bf16[4,256,256]{2,1,0:T(8,128)(2,1)S(1)}, bf16[4,256,256]{...) custom-call(s32[1,1,5]{2,1,0:T(1,128)} %mix.1, ...), custom_call_target="tpu_custom_call" | custom-call | tf_op jit(solution)/shard_map/gossip_step/pallas_call | solution.py:608
  78.9 3.6 %finish.1 = (f32[256,4096]{1,0:T(8,128)}, f32[256,1024]{1,0:T(8,128)}, f32[256,1024]{1,0:T(8,128)}, f32[256,1024]{1,0:T(8,128)}, f32[1,1,256]{2,1,0:T(1,128)}, /...) custom-call(bf16[4,256,256]{2,1,0:T(8,128)(2,1)S(1)} %get-tuple-element.27.ur0, ...), custom_call_target="tpu_custom_call" | custom-call | tf_op jit(solution)/shard_map/finish/pallas_call | solution.py:650

commit v4 on v3

--- a/solution.py
+++ b/solution.py
@@ -16,19 +16,19 @@
 WROWS = BLK + 16
 
 VG = 0
-WL = 6
-WR = 14
-NS = 22
-US = 34
-RR = 46
-RL = 54
-GG = 62
-GO = 65
-NSEM = 70
+WL = 12
+WR = 28
+NS = 44
+US = 56
+RR = 68
+RL = 76
+GG = 84
+GO = 87
+NSEM = 94
 
 
 def KC(k):
-    for lo, c in ((65, "GO"), (62, "GG"), (46, "RS"), (34, "US"), (22, "NS"), (6, "W"), (0, "VG")):
+    for lo, c in ((87, "GO"), (84, "GG"), (68, "RS"), (56, "US"), (44, "NS"), (12, "W"), (0, "VG")):
         if k >= lo:
             return c
 
@@ -96,22 +96,6 @@
     for c in loads:
         c.start()
 
-    pl.semaphore_wait(barrier, len(partners))
-
-    sent = []
-
-    def go(copy, cond=None):
-        copy.start()
-        sent.append((cond, copy))
-
-    def half(ref, slot, h):
-        return ref.at[pl.ds(slot * ROWS + h * (ROWS // 2), ROWS // 2)]
-
-    go(remote(half(vg_hbm, 0, 0), half(vgp, 1, 0), VG + 0, ypeer(1)))
-    go(remote(half(vg_hbm, 0, 1), half(vgp, 3, 1), VG + 1, ypeer(3)))
-    go(remote(half(vg_hbm, 0, 1), half(vgp, 1, 1), VG + 2, ypeer(1)))
-    go(remote(half(vg_hbm, 0, 0), half(vgp, 3, 0), VG + 3, ypeer(3)))
-
     loads[0].wait()
     gain_row = gain[0].astype(BF16)
 
@@ -124,25 +108,52 @@
     wp[z, BLK:WROWS, :] = jnp.zeros((16, KV), BF16)
     wp[z, BLK:WROWS, 0:BLK] = jnp.broadcast_to(gain_row.astype(F32), (16, BLK)).astype(BF16)
 
-    def whalf(block, h):
-        return wp.at[block, pl.ds(h * 128, 128 + 16 * h)]
-
-    def wright(s, h):
-        return remote(whalf(z - s, h), whalf(z - s, h), WL + 2 * s + h, dev(y, z + 1))
-
-    def wleft(s, h):
-        return remote(whalf(z + s, h), whalf(z + s, h), WR + 2 * s + h, dev(y, z - 1))
-
-    def from_left(s, h):
-        remote(whalf(z - s, h), whalf(z - s, h), WL + 2 * s + h - 2, dev(y, z)).wait_recv()
-
-    def from_right(s, h):
-        remote(whalf(z + s, h), whalf(z + s, h), WR + 2 * s + h - 2, dev(y, z)).wait_recv()
-
-    def far(zz, h):
-        return remote(
-            whalf(zz, h), gos.at[3, pl.ds(h * 128, 128 + 16 * h)], GO + 3 + h,
-            (far_rx, ry, y * 4 + zz))
+    pl.semaphore_wait(barrier, len(partners))
+
+    sent = []
+
+    def go(copy, cond=None):
+        copy.start()
+        sent.append((cond, copy))
+
+    def half(ref, slot, h, c):
+        return ref.at[pl.ds(slot * ROWS + h * (ROWS // 2), ROWS // 2), pl.ds(c * (KV // 2), KV // 2)]
+
+    def vg_own(c):
+        for k, (r, h) in enumerate(((1, 0), (3, 1), (1, 1), (3, 0))):
+            go(remote(half(vg_hbm, 0, h, c), half(vgp, r, h, c), VG + 6 * c + k, ypeer(r)))
+
+    def vg_arrived(c, k, slot, h):
+        remote(half(vgp, slot, h, c), half(vgp, slot, h, c), VG + 6 * c + k, ypeer(1)).wait_recv()
+
+    def vg_relay(c):
+        for k, (r, h) in enumerate(((1, 0), (3, 1))):
+            vg_arrived(c, k, r, h)
+            go(remote(half(vgp, r, h, c), half(vgp, 2, h, c), VG + 6 * c + 4 + k, ypeer(r)))
+
+    def vg_all(c):
+        for k, (r, h) in ((2, (1, 1)), (3, (3, 0)), (4, (2, 0)), (5, (2, 1))):
+            vg_arrived(c, k, r, h)
+
+    vg_own(0)
+
+    def quarter(ref, block, q):
+        return ref.at[block, pl.ds(q * 64, 64 + 16 * (q // 3))]
+
+    def wright(s, q):
+        return remote(quarter(wp, z - s, q), quarter(wp, z - s, q), WL + 4 * s + q, dev(y, z + 1))
+
+    def wleft(s, q):
+        return remote(quarter(wp, z + s, q), quarter(wp, z + s, q), WR + 4 * s + q, dev(y, z - 1))
+
+    def from_left(s, q):
+        remote(quarter(wp, z - s, q), quarter(wp, z - s, q), WL + 4 * s + q - 4, dev(y, z)).wait_recv()
+
+    def from_right(s, q):
+        remote(quarter(wp, z + s, q), quarter(wp, z + s, q), WR + 4 * s + q - 4, dev(y, z)).wait_recv()
+
+    def far(zz, q):
+        return remote(quarter(wp, zz, q), quarter(gos, 3, q), GO + 3 + q, (far_rx, ry, y * 4 + zz))
 
     @pl.when(z < 3)
     def _():
@@ -154,15 +165,20 @@
 
     @pl.when(z < 2)
     def _():
-        wright(0, 1).start()
+        for q in (1, 2, 3):
+            wright(0, q).start()
 
     @pl.when(z > 1)
     def _():
-        wleft(0, 1).start()
+        for q in (1, 2, 3):
+            wleft(0, q).start()
 
     go(remote(wp.at[z], gos.at[2], GO + 2, (chip_rx, ry, f)))
     go(remote(wp.at[z], gos.at[0], GO + 0, (rx, (ry + 1) % 4, f)))
     go(remote(wp.at[z], gos.at[1], GO + 1, (rx, (ry + 3) % 4, f)))
+
+    vg_relay(0)
+    vg_own(1)
 
     loads[1].wait()
 
@@ -184,20 +200,18 @@
 
     lax.fori_loop(0, ROWS // 64, norm_rows, 0)
 
-    remote(half(vg_hbm, 0, 0), half(vgp, 1, 0), VG + 0, ypeer(1)).wait_recv()
-    go(remote(half(vgp, 1, 0), half(vgp, 2, 0), VG + 4, ypeer(1)))
-    remote(half(vg_hbm, 0, 1), half(vgp, 3, 1), VG + 1, ypeer(3)).wait_recv()
-    go(remote(half(vgp, 3, 1), half(vgp, 2, 1), VG + 5, ypeer(3)))
-
-    @pl.when(z == 2)
-    def _():
-        from_left(1, 0)
-        wright(1, 0).start()
-
-    @pl.when(z == 1)
-    def _():
-        from_right(1, 0)
-        wleft(1, 0).start()
+    def outwards(q):
+        @pl.when(z == 2)
+        def _():
+            from_left(1, q)
+            wright(1, q).start()
+
+        @pl.when(z == 1)
+        def _():
+            from_right(1, q)
+            wleft(1, q).start()
+
+    outwards(0)
 
     def order(i):
         return grad_order(z, i)
@@ -209,9 +223,8 @@
         b = order(i)
         return remote(nown.at[(y + r) % 4, b], npool.at[b, slot(r)], NS + 3 * i + r - 1, ypeer(r))
 
-    for i in range(4):
-        for r in (1, 3, 2):
-            go(ncopy(i, r))
+    for r in (1, 3, 2):
+        go(ncopy(0, r))
 
     def own_rows(i, carry):
         rows = pl.ds(pl.multiple_of(i * 64, 64), 64)
@@ -221,50 +234,54 @@
 
     lax.fori_loop(0, ROWS // 64, own_rows, 0)
 
-    def half_rows(h):
-        return pl.ds(h * 128, 128)
-
-    def rsright(b, h):
-        return remote(rsend.at[b, half_rows(h)], rr.at[b, half_rows(h)], RR + 2 * b + h, dev(y, z + 1))
-
-    def rsleft(b, h):
-        return remote(rsend.at[b, half_rows(h)], rl.at[b, half_rows(h)], RL + 2 * b + h, dev(y, z - 1))
-
-    def round_half(b, h, other=None):
+    def part(ref, b, c):
+        return ref.at[b, :, pl.ds(c * (KV // 2), KV // 2)]
+
+    def rsright(b, c):
+        return remote(part(rsend, b, c), part(rr, b, c), RR + 2 * b + c, dev(y, z + 1))
+
+    def rsleft(b, c):
+        return remote(part(rsend, b, c), part(rl, b, c), RL + 2 * b + c, dev(y, z - 1))
+
+    def sums_in(b, c, ref, k):
+        remote(part(rsend, b, c), part(ref, b, c), k + 2 * b + c, dev(y, z)).wait_recv()
+
+    def round_half(b, c, other=None):
+        cols = pl.ds(c * (KV // 2), KV // 2)
+
         def rows_body(i, carry):
-            rows = pl.ds(pl.multiple_of(h * 128 + i * 32, 32), 32)
-            g = gbuf[b, rows, :]
+            rows = pl.ds(pl.multiple_of(i * 32, 32), 32)
+            g = gbuf[b, rows, cols]
             if other is not None:
-                g = g + other[b, rows, :].astype(F32)
-            rsend[b, rows, :] = g.astype(BF16)
+                g = g + other[b, rows, cols].astype(F32)
+            rsend[b, rows, cols] = g.astype(BF16)
             return carry
 
-        lax.fori_loop(0, 4, rows_body, 0)
-
-    def weight_grad(i):
+        lax.fori_loop(0, BLK // 32, rows_body, 0)
+
+    def weight_grad(i, c):
         b = order(i)
-        for r in (1, 3, 2):
-            ncopy(i, r).wait_recv()
-        npt[...] = npool[b].T
-
-        def columns(c, carry):
-            cols = pl.ds(pl.multiple_of(c * 256, 256), 256)
+        if c == 0:
+            for r in (1, 3, 2):
+                ncopy(i, r).wait_recv()
+            npt[...] = npool[b].T
+
+        def columns(k, carry):
+            cols = pl.ds(pl.multiple_of(c * (KV // 2) + k * 256, 256), 256)
             gbuf[b, :, cols] = jnp.dot(npt[...], vgp[:, cols], preferred_element_type=F32)
             return carry
 
-        lax.fori_loop(0, KV // 256, columns, 0)
+        lax.fori_loop(0, KV // 512, columns, 0)
         if i < 3:
             @pl.when(z == 0)
             def _():
-                for h in (0, 1):
-                    round_half(3 - i, h)
-                    rsright(3 - i, h).start()
+                round_half(3 - i, c)
+                rsright(3 - i, c).start()
 
             @pl.when(z == 3)
             def _():
-                for h in (0, 1):
-                    round_half(i, h)
-                    rsleft(i, h).start()
+                round_half(i, c)
+                rsleft(i, c).start()
 
     def ucopy(i, r):
         b = unit_order(z, i)
@@ -305,49 +322,35 @@
         gg[b] = jnp.sum(spread.reshape(BLK // 8, 8, BLK), axis=0)
 
     def relay_right(s):
-        for h in (0, 1):
-            from_left(s, h)
-            wright(s, h).start()
+        for q in range(4):
+            from_left(s, q)
+            wright(s, q).start()
 
     def relay_left(s):
-        for h in (0, 1):
-            from_right(s, h)
-            wleft(s, h).start()
-
-    @pl.when(z == 2)
-    def _():
-        from_left(1, 1)
-        wright(1, 1).start()
-        wright(0, 1).start()
-        relay_left(1)
-
-    @pl.when(z == 1)
-    def _():
-        from_right(1, 1)
-        wleft(1, 1).start()
-        wleft(0, 1).start()
-        relay_right(1)
-
-    def gossip_out(s, h):
+        for q in range(4):
+            from_right(s, q)
+            wleft(s, q).start()
+
+    def gossip_out(s, q):
         @pl.when(z == 3)
         def _():
-            from_left(s, h)
-            far(3 - s, h).start()
+            from_left(s, q)
+            far(3 - s, q).start()
 
         @pl.when(z == 0)
         def _():
-            from_right(s, h)
-            far(s, h).start()
-
-    def forward_right(b, h):
-        remote(rsend.at[b, half_rows(h)], rr.at[b, half_rows(h)], RR + 2 * b + h, dev(y, z)).wait_recv()
-        round_half(b, h, rr)
-        rsright(b, h).start()
-
-    def forward_left(b, h):
-        remote(rsend.at[b, half_rows(h)], rl.at[b, half_rows(h)], RL + 2 * b + h, dev(y, z)).wait_recv()
-        round_half(b, h, rl)
-        rsleft(b, h).start()
+            from_right(s, q)
+            far(s, q).start()
+
+    def forward_right(b, c):
+        sums_in(b, c, rr, RR)
+        round_half(b, c, rr)
+        rsright(b, c).start()
+
+    def forward_left(b, c):
+        sums_in(b, c, rl, RL)
+        round_half(b, c, rl)
+        rsleft(b, c).start()
 
     def forward_first(h):
         @pl.when(z == 1)
@@ -369,13 +372,36 @@
             forward_right(3, h)
             forward_left(1, h)
 
+    outwards(1)
     gossip_out(2, 0)
+    vg_relay(1)
+    for i in (1, 2, 3):
+        for r in (1, 3, 2):
+            go(ncopy(i, r))
+    outwards(2)
+    gossip_out(2, 1)
+    outwards(3)
+    gossip_out(2, 2)
+
+    @pl.when(z == 2)
+    def _():
+        for q in (1, 2, 3):
+            wright(0, q).start()
+        relay_left(1)
+
+    @pl.when(z == 1)
+    def _():
+        for q in (1, 2, 3):
+            wleft(0, q).start()
+        relay_right(1)
+
     loads[2].wait()
-    for k, (s, h) in ((4, (2, 0)), (5, (2, 1)), (2, (1, 1)), (3, (3, 0))):
-        remote(half(vgp, s, h), half(vgp, s, h), VG + k, ypeer(1)).wait_recv()
-    gossip_out(2, 1)
+    gossip_out(2, 3)
+    vg_all(0)
+    weight_grad(0, 0)
+    vg_all(1)
+    weight_grad(0, 1)
     unit_grad(0)
-    weight_grad(0)
 
     @pl.when(z == 2)
     def _():
@@ -386,26 +412,29 @@
         relay_left(2)
 
     unit_grad(1)
-    weight_grad(1)
+    weight_grad(1, 0)
+    weight_grad(1, 1)
     forward_first(0)
 
     @pl.when(z == 3)
     def _():
-        from_left(1, 0)
-        from_left(1, 1)
+        for q in range(4):
+            from_left(1, q)
 
     @pl.when(z == 0)
     def _():
-        from_right(1, 0)
-        from_right(1, 1)
+        for q in range(4):
+            from_right(1, q)
 
     unit_grad(2)
-    weight_grad(2)
-    gossip_out(3, 0)
-    gossip_out(3, 1)
+    weight_grad(2, 0)
+    weight_grad(2, 1)
+    for q in range(4):
+        gossip_out(3, q)
     forward_first(1)
     unit_grad(3)
-    weight_grad(3)
+    weight_grad(3, 0)
+    weight_grad(3, 1)
     forward_second(0)
 
     def gain_block(b, carry):
@@ -444,10 +473,9 @@
     remote(gos.at[2], gos.at[2], GO + 2, dev(y, z)).wait_recv()
     remote(gos.at[0], gos.at[0], GO + 0, dev(y, z)).wait_recv()
     remote(gos.at[1], gos.at[1], GO + 1, dev(y, z)).wait_recv()
-    far_in = gos.at[3, pl.ds(0, 128)]
-    remote(far_in, far_in, GO + 3, dev(y, z)).wait_recv()
-    far_in = gos.at[3, pl.ds(128, 144)]
-    remote(far_in, far_in, GO + 4, dev(y, z)).wait_recv()
+    for q in range(4):
+        far_in = quarter(gos, 3, q)
+        remote(far_in, far_in, GO + 3 + q, dev(y, z)).wait_recv()
 
     def gossip_gain(n):
         return gos[n, BLK:WROWS, 0:BLK].astype(F32)[0:1, :]
@@ -470,22 +498,37 @@
 
     loads[3].wait()
     loads[4].wait()
-    s0, s1, s2 = share(0, KV), share(3, KV), share(4, KV)
-    s3, s4 = share(from_chip, KV), share(from_far, KV)
-
-    def adam_rows(i, carry):
-        rows = pl.ds(pl.multiple_of(i * 32, 32), 32)
-        g = gbuf[z, rows, :] + rr[z, rows, :].astype(F32) + rl[z, rows, :].astype(F32)
-        g = gcol[rows, 0:1] * g
-        new_m = 0.9 * mv[rows, :] + 0.1 * g
-        new_v = 0.999 * vv[rows, :] + 0.001 * g * g
-        nm[rows, :] = new_m
-        nv[rows, :] = new_v
-        own = wf[rows, :]
-        stepped = own - 0.01 * (new_m / (jnp.sqrt(new_v) + 1e-08) + 0.1 * own)
-        out = s0 * stepped + s1 * gos[0, rows, :].astype(F32) + s2 * gos[1, rows, :].astype(F32)
-        nw[rows, :] = out + s3 * gos[2, rows, :].astype(F32) + s4 * gos[3, rows, :].astype(F32)
-        return carry
+    s0, s1, s2 = share(0, KV // 2), share(3, KV // 2), share(4, KV // 2)
+    s3, s4 = share(from_chip, KV // 2), share(from_far, KV // 2)
+
+    for c in (0, 1):
+        cols = pl.ds(c * (KV // 2), KV // 2)
+
+        def mix_rows(i, carry):
+            rows = pl.ds(pl.multiple_of(i * 32, 32), 32)
+            own = wf[rows, cols]
+            out = s0 * (own - 0.01 * (0.1 * own))
+            out = out + s1 * gos[0, rows, cols].astype(F32) + s2 * gos[1, rows, cols].astype(F32)
+            nw[rows, cols] = out + s3 * gos[2, rows, cols].astype(F32) + s4 * gos[3, rows, cols].astype(F32)
+            return carry
+
+        lax.fori_loop(0, BLK // 32, mix_rows, 0)
+
+    def adam(c):
+        cols = pl.ds(c * (KV // 2), KV // 2)
+
+        def adam_rows(i, carry):
+            rows = pl.ds(pl.multiple_of(i * 32, 32), 32)
+            g = gbuf[z, rows, cols] + rr[z, rows, cols].astype(F32) + rl[z, rows, cols].astype(F32)
+            g = gcol[rows, 0:1] * g
+            new_m = 0.9 * mv[rows, cols] + 0.1 * g
+            new_v = 0.999 * vv[rows, cols] + 0.001 * g * g
+            nm[rows, cols] = new_m
+            nv[rows, cols] = new_v
+            nw[rows, cols] = nw[rows, cols] - s0 * (0.01 * (new_m / (jnp.sqrt(new_v) + 1e-08)))
+            return carry
+
+        lax.fori_loop(0, BLK // 32, adam_rows, 0)
 
     def add_inner(i):
         for r in (1, 3, 2):
@@ -503,25 +546,25 @@
 
         lax.fori_loop(0, ROWS // 64, rows_body, 0)
 
-    for h in (0, 1):
-        add_inner(h)
+    for c in (0, 1):
+        add_inner(c)
 
         @pl.when(z > 0)
         def _():
-            remote(rsend.at[z, half_rows(h)], rr.at[z, half_rows(h)], RR + 2 * z + h, dev(y, z)).wait_recv()
+            sums_in(z, c, rr, RR)
 
         @pl.when(z < 3)
         def _():
-            remote(rsend.at[z, half_rows(h)], rl.at[z, half_rows(h)], RL + 2 * z + h, dev(y, z)).wait_recv()
-
-        lax.fori_loop(4 * h, 4 * h + 4, adam_rows, 0)
+            sums_in(z, c, rl, RL)
+
+        adam(c)
 
     add_inner(2)
     add_inner(3)
 
     for _, copy in sent:
         copy.wait_send()
-    for h in (0, 1):
+    for q in range(4):
         for s, right, left in (
             (0, z < 3, z > 0),
             (1, (z == 1) | (z == 2), (z == 1) | (z == 2)),
@@ -529,21 +572,22 @@
         ):
             @pl.when(right)
             def _():
-                wright(s, h).wait_send()
+                wright(s, q).wait_send()
 
             @pl.when(left)
             def _():
-                wleft(s, h).wait_send()
+                wleft(s, q).wait_send()
 
         for s in (2, 3):
             @pl.when(z == 3)
             def _():
-                far(3 - s, h).wait_send()
+                far(3 - s, q).wait_send()
 
             @pl.when(z == 0)
             def _():
-                far(s, h).wait_send()
-
+                far(s, q).wait_send()
+
+    for h in (0, 1):
         for b in range(4):
             @pl.when(z < b)
             def _():

time: 82.6 us -> 81.3 us (0.984)
  Pallas kernels: 81.9 us -> 80.6 us
    pallas_call x1, Pallas kernels: 78.3 us -> 77 us  [body(): pl.pallas_call(step_kernel, name='gossip_step', out_shape=[pltpu.VMEM(*a)...]
where the time goes in v4:
time: 81.3 us; the launch traced here: 81.2 us
  Pallas kernels  80.6 us (99%)
    pallas_call x1, Pallas kernels, body(): pl.pallas_call(step_kernel, name='gossip_step', out_shape=[pltpu.VMEM(*a)...  77 us
    pallas_call x1, Pallas kernels, body(): pl.pallas_call(finish_kernel, name='finish', out_shape=[jax.ShapeDtypeStr...  3.62 us

profile of v4, /device:TPU:1, one launch (start us, length us, event | category | flops | bytes accessed | tf_op | source)
XLA Modules:
  0.0 81.2 jit_solution(791833578416296110)
XLA Ops:
  0.6 77.0 %gossip_step.1 = (bf16[4,256,256]{2,1,0:T(8,128)(2,1)S(1)}, bf16[4,256,256]{2,1,0:T(8,128)(2,1)S(1)}, bf16[4,256,256]{2,1,0:T(8,128)(2,1)S(1)}, bf16[4,256,256]{...) custom-call(s32[1,1,5]{2,1,0:T(1,128)} %mix.1, ...), custom_call_target="tpu_custom_call" | custom-call | tf_op jit(solution)/shard_map/gossip_step/pallas_call | solution.py:652
  77.6 3.6 %finish.1 = (f32[256,4096]{1,0:T(8,128)}, f32[256,1024]{1,0:T(8,128)}, f32[256,1024]{1,0:T(8,128)}, f32[256,1024]{1,0:T(8,128)}, f32[1,1,256]{2,1,0:T(1,128)}, /...) custom-call(bf16[4,256,256]{2,1,0:T(8,128)(2,1)S(1)} %get-tuple-element.27.ur0, ...), custom_call_target="tpu_custom_call" | custom-call | tf_op jit(solution)/shard_map/finish/pallas_call | solution.py:694

commit v5 on v4

--- a/solution.py
+++ b/solution.py
@@ -93,8 +93,39 @@
         pltpu.make_async_copy(m_hbm, mv, lsem.at[3]),
         pltpu.make_async_copy(v_hbm, vv, lsem.at[4]),
     ]
-    for c in loads:
-        c.start()
+    for k in (0, 1):
+        loads[k].start()
+
+    pl.semaphore_wait(barrier, len(partners))
+
+    sent, sent_units = [], []
+
+    def go(copy, to=sent):
+        copy.start()
+        to.append(copy)
+
+    def half(ref, slot, h, c):
+        return ref.at[pl.ds(slot * ROWS + h * (ROWS // 2), ROWS // 2), pl.ds(c * (KV // 2), KV // 2)]
+
+    def vg_own(c):
+        for k, (r, h) in enumerate(((1, 0), (3, 1), (1, 1), (3, 0))):
+            go(remote(half(vg_hbm, 0, h, c), half(vgp, r, h, c), VG + 6 * c + k, ypeer(r)))
+
+    def vg_arrived(c, k, slot, h):
+        remote(half(vgp, slot, h, c), half(vgp, slot, h, c), VG + 6 * c + k, ypeer(1)).wait_recv()
+
+    def vg_relay(c):
+        for k, (r, h) in enumerate(((1, 0), (3, 1))):
+            vg_arrived(c, k, r, h)
+            go(remote(half(vgp, r, h, c), half(vgp, 2, h, c), VG + 6 * c + 4 + k, ypeer(r)))
+
+    def vg_all(c):
+        for k, (r, h) in ((2, (1, 1)), (3, (3, 0)), (4, (2, 0)), (5, (2, 1))):
+            vg_arrived(c, k, r, h)
+
+    vg_own(0)
+    for k in (2, 3, 4):
+        loads[k].start()
 
     loads[0].wait()
     gain_row = gain[0].astype(BF16)
@@ -108,34 +139,6 @@
     wp[z, BLK:WROWS, :] = jnp.zeros((16, KV), BF16)
     wp[z, BLK:WROWS, 0:BLK] = jnp.broadcast_to(gain_row.astype(F32), (16, BLK)).astype(BF16)
 
-    pl.semaphore_wait(barrier, len(partners))
-
-    sent = []
-
-    def go(copy, cond=None):
-        copy.start()
-        sent.append((cond, copy))
-
-    def half(ref, slot, h, c):
-        return ref.at[pl.ds(slot * ROWS + h * (ROWS // 2), ROWS // 2), pl.ds(c * (KV // 2), KV // 2)]
-
-    def vg_own(c):
-        for k, (r, h) in enumerate(((1, 0), (3, 1), (1, 1), (3, 0))):
-            go(remote(half(vg_hbm, 0, h, c), half(vgp, r, h, c), VG + 6 * c + k, ypeer(r)))
-
-    def vg_arrived(c, k, slot, h):
-        remote(half(vgp, slot, h, c), half(vgp, slot, h, c), VG + 6 * c + k, ypeer(1)).wait_recv()
-
-    def vg_relay(c):
-        for k, (r, h) in enumerate(((1, 0), (3, 1))):
-            vg_arrived(c, k, r, h)
-            go(remote(half(vgp, r, h, c), half(vgp, 2, h, c), VG + 6 * c + 4 + k, ypeer(r)))
-
-    def vg_all(c):
-        for k, (r, h) in ((2, (1, 1)), (3, (3, 0)), (4, (2, 0)), (5, (2, 1))):
-            vg_arrived(c, k, r, h)
-
-    vg_own(0)
 
     def quarter(ref, block, q):
         return ref.at[block, pl.ds(q * 64, 64 + 16 * (q // 3))]
@@ -300,8 +303,8 @@
             return carry
 
         lax.fori_loop(0, 4, tokens, 0)
-        for r in (1, 3, 2):
-            go(ucopy(i, r))
+        for r in (2, 1, 3):
+            go(ucopy(i, r), sent_units)
         ur[i][y] = us[b, 0:ROWS, :]
 
     eye = lax.broadcasted_iota(jnp.int32, (BLK, BLK), 0) == lax.broadcasted_iota(jnp.int32, (BLK, BLK), 1)
@@ -559,10 +562,7 @@
 
         adam(c)
 
-    add_inner(2)
-    add_inner(3)
-
-    for _, copy in sent:
+    for copy in sent:
         copy.wait_send()
     for q in range(4):
         for s, right, left in (
@@ -596,6 +596,13 @@
             @pl.when(z > b)
             def _():
                 rsleft(b, h).wait_send()
+
+    add_inner(2)
+    for copy in sent_units[:9]:
+        copy.wait_send()
+    add_inner(3)
+    for copy in sent_units[9:]:
+        copy.wait_send()
 
 
 def finish_kernel(

time: 81.3 us -> 80.8 us (level)
  no operation moved by 1% of the time
where the time goes in v5:
time: 80.8 us; the launch traced here: 80.7 us
  Pallas kernels  80 us (99%)
    pallas_call x1, Pallas kernels, body(): pl.pallas_call(step_kernel, name='gossip_step', out_shape=[pltpu.VMEM(*a)...  76.4 us
    pallas_call x1, Pallas kernels, body(): pl.pallas_call(finish_kernel, name='finish', out_shape=[jax.ShapeDtypeStr...  3.62 us

profile of v5, /device:TPU:1, one launch (start us, length us, event | category | flops | bytes accessed | tf_op | source)
XLA Modules:
  0.0 80.7 jit_solution(3160055455199805303)
XLA Ops:
  0.6 76.4 %gossip_step.1 = (bf16[4,256,256]{2,1,0:T(8,128)(2,1)S(1)}, bf16[4,256,256]{2,1,0:T(8,128)(2,1)S(1)}, bf16[4,256,256]{2,1,0:T(8,128)(2,1)S(1)}, bf16[4,256,256]{...) custom-call(s32[1,1,5]{2,1,0:T(1,128)} %mix.1, ...), custom_call_target="tpu_custom_call" | custom-call | tf_op jit(solution)/shard_map/gossip_step/pallas_call | solution.py:659
  77.0 3.6 %finish.1 = (f32[256,4096]{1,0:T(8,128)}, f32[256,1024]{1,0:T(8,128)}, f32[256,1024]{1,0:T(8,128)}, f32[256,1024]{1,0:T(8,128)}, f32[1,1,256]{2,1,0:T(1,128)}, /...) custom-call(bf16[4,256,256]{2,1,0:T(8,128)(2,1)S(1)} %get-tuple-element.27.ur0, ...), custom_call_target="tpu_custom_call" | custom-call | tf_op jit(solution)/shard_map/finish/pallas_call | solution.py:701

commit v6 on v5

--- a/solution.py
+++ b/solution.py
@@ -181,7 +181,6 @@
     go(remote(wp.at[z], gos.at[1], GO + 1, (rx, (ry + 3) % 4, f)))
 
     vg_relay(0)
-    vg_own(1)
 
     loads[1].wait()
 
@@ -228,6 +227,7 @@
 
     for r in (1, 3, 2):
         go(ncopy(0, r))
+    vg_own(1)
 
     def own_rows(i, carry):
         rows = pl.ds(pl.multiple_of(i * 64, 64), 64)
@@ -377,14 +377,14 @@
 
     outwards(1)
     gossip_out(2, 0)
+    outwards(2)
+    gossip_out(2, 1)
+    outwards(3)
+    gossip_out(2, 2)
     vg_relay(1)
     for i in (1, 2, 3):
         for r in (1, 3, 2):
             go(ncopy(i, r))
-    outwards(2)
-    gossip_out(2, 1)
-    outwards(3)
-    gossip_out(2, 2)
 
     @pl.when(z == 2)
     def _():

time: 80.8 us -> 80.7 us (level)
  no operation moved by 1% of the time
where the time goes in v6:
time: 80.7 us; the launch traced here: 80.6 us
  Pallas kernels  80 us (99%)
    pallas_call x1, Pallas kernels, body(): pl.pallas_call(step_kernel, name='gossip_step', out_shape=[pltpu.VMEM(*a)...  76.4 us
    pallas_call x1, Pallas kernels, body(): pl.pallas_call(finish_kernel, name='finish', out_shape=[jax.ShapeDtypeStr...  3.62 us

profile of v6, /device:TPU:1, one launch (start us, length us, event | category | flops | bytes accessed | tf_op | source)
XLA Modules:
  0.0 80.6 jit_solution(7401898166436315152)
XLA Ops:
  0.6 76.4 %gossip_step.1 = (bf16[4,256,256]{2,1,0:T(8,128)(2,1)S(1)}, bf16[4,256,256]{2,1,0:T(8,128)(2,1)S(1)}, bf16[4,256,256]{2,1,0:T(8,128)(2,1)S(1)}, bf16[4,256,256]{...) custom-call(s32[1,1,5]{2,1,0:T(1,128)} %mix.1, ...), custom_call_target="tpu_custom_call" | custom-call | tf_op jit(solution)/shard_map/gossip_step/pallas_call | solution.py:659
  77.0 3.6 %finish.1 = (f32[256,4096]{1,0:T(8,128)}, f32[256,1024]{1,0:T(8,128)}, f32[256,1024]{1,0:T(8,128)}, f32[256,1024]{1,0:T(8,128)}, f32[1,1,256]{2,1,0:T(1,128)}, /...) custom-call(bf16[4,256,256]{2,1,0:T(8,128)(2,1)S(1)} %get-tuple-element.27.ur0, ...), custom_call_target="tpu_custom_call" | custom-call | tf_op jit(solution)/shard_map/finish/pallas_call | solution.py:701
